TPU v7x, 256 devices: a whole 4x4x8 slice. The times are simulated.
256 devices in a mesh: row: 8 (over z), col: 32 (over y, x, core).
Axes of the slice: x: 4, y: 4, z: 8, core: 2. Of those that a mesh axis runs over, the one named last changes fastest.
Arguments:
- transitions: bfloat16 [16384, 16384], P('row', 'col'), as said below
- forward: bfloat16 [2, 16384, 512], P(None, 'row'), may hold values from 0.02 to 3
- emission: bfloat16 [2, 16384, 512], P(None, ('row', 'col')), may hold values from 0.01 to 1
- beta_end: float32 [16384, 512], P(('row', 'col')), may hold values from 0.2 to 5
- token_ids: int32 [2, 512], replicated, may hold values from 0 to 50256, as said below
Outputs:
- counts: float32 [16384, 16384], P('row', 'col')
- beta_start: float32 [16384, 512], P(('row', 'col'))
- log_scales: float32 [2, 512], replicated
Inputs may be any that keep to these rules, and one draw needn't show every extreme that they name: `token_ids`: the id 50257 - 1 marks a step past the end of the sequence; once a sequence has ended, every later step of it has that id. `transitions`: every entry is positive.
All inputs are finite; a program needn't handle non-finite values.
Results may differ from a plain program's by a relative error of at most 0.00033.
Values may be sent and summed in bfloat16 or wider, within the bound.
No kernel may reach another device: no remote copies, remote signals or barrier semaphores. Data moves between devices by JAX's collectives and lax.ppermute only.
A program may use at most 64 MiB of HBM per device.

v0:
```python
import jax
import jax.numpy as jnp
from jax import lax
from jax.sharding import PartitionSpec as P

VOCAB = 50257


def global_totals(weighted, plain):
    return lax.psum((weighted, plain), ("row", "col"))


def local(transitions, forward, emission, beta_end, token_ids):
    states_all = transitions.shape[1] * lax.axis_size("col")
    piece = beta_end.shape[0]
    seqs = beta_end.shape[1]
    steps = forward.shape[0]
    offset = lax.axis_index("col") * piece
    beta = beta_end
    post_list = []
    weight_list = []
    log_list = [None] * steps
    for step in reversed(range(steps)):
        ended = token_ids[step] == states_all * 0 + VOCAB - 1
        observed = jnp.where(ended[None, :], jnp.float32(1.0), emission[step].astype(jnp.float32))
        weights = (observed * beta).astype(jnp.bfloat16)
        weights_col = lax.all_gather(weights, "row", axis=0, tiled=True)
        alpha_block = forward[step]
        alpha_piece = lax.dynamic_slice_in_dim(alpha_block, offset, piece, 0).astype(jnp.float32)
        raw = lax.psum_scatter(
            jnp.dot(transitions, weights_col, preferred_element_type=jnp.float32) / states_all,
            "col",
            scatter_dimension=0,
            tiled=True,
        )
        totals = global_totals(jnp.sum(alpha_piece * raw, axis=0), jnp.sum(raw, axis=0))
        norm = totals[0] / states_all
        scale = totals[1] / states_all
        post_list.append((alpha_block.astype(jnp.float32) / norm[None, :]).astype(jnp.bfloat16))
        weight_list.append(weights_col)
        log_list[step] = jnp.log(scale)
        beta = raw / scale[None, :]
    posts = jnp.concatenate(post_list, axis=1)
    wcols = jnp.concatenate(weight_list, axis=1)
    mixed = lax.dot_general(
        posts, wcols, (((1,), (1,)), ((), ())), preferred_element_type=jnp.float32
    )
    counts = transitions.astype(jnp.float32) * mixed / seqs
    return (counts, beta, jnp.stack(log_list))


def solution(mesh):
    in_specs = (
        P("row", "col"),
        P(None, "row", None),
        P(None, ("row", "col"), None),
        P(("row", "col"), None),
        P(),
    )
    out_specs = (P("row", "col"), P(("row", "col"), None), P())
    return jax.shard_map(local, mesh=mesh, in_specs=in_specs, out_specs=out_specs, check_vma=False)
```

profile of v0, /device:TPU:1, one launch (start us, length us, event | category | flops | bytes accessed | tf_op | source)
XLA Modules:
  0.0 435.5 jit_solution(10268991113844791204)
XLA Ops:
  7.2 0.0 reduce-scatter.7.cloned.1.call-start
  7.2 0.8 compare_reduce_fusion
  8.0 0.9 fusion.16
  8.9 23.7 %all_gather.6 = bf16[512,512]{1,0:T(8,128)(2,1)S(1)} all-gather(bf16[64,512]{1,0:T(8,128)(2,1)S(1)} %fusion.16), channel_id=1, replica_groups=mesh['row'=8,'col'=32] {'row'}, dimensions={0}, use_global_device_ids=true | all-gather | bytes 589824 | tf_op jit(solution)/shard_map/all_gather | solution.py:27
  32.7 4.9 %multiply_bitcast_fusion.1 = f32[2048,512]{0,1:T(8,128)} fusion(bf16[512,512]{1,0:T(8,128)(2,1)S(1)} %all_gather.6, bf16[2048,512]{1,0:T(8,128)(2,1)} %param.5), kind=kOutput, calls=%fused_computation.10 | convolution fusion | flops 1074790400 | bytes 6815744 | tf_op jit(solution)/shard_map/dot_general | solution.py:31
  37.6 5.3 %copy.18 = f32[2048,512]{1,0:T(8,128)} copy(f32[2048,512]{0,1:T(8,128)} %multiply_bitcast_fusion.1) | data formatting | bytes 8388608
  42.9 0.0 copy-start.2
  42.9 0.0 copy-start
  42.9 0.0 reduce-scatter.7.cloned.1.call-update
  43.0 0.0 reduce-scatter.9.cloned.1.call-start
  43.0 93.4 %reduce-scatter.7.cloned.1.call-done = f32[64,512]{1,0:T(8,128)} async-done(((f32[2048,512]{1,0:T(8,128)}), f32[64,512]{1,0:T(8,128)}) %reduce-scatter.7.cloned.1.call-update) | async-done | bytes 131088 | tf_op jit(solution)/shard_map/reduce_scatter | solution.py:30
  136.4 0.9 reduce_sum.37
  137.3 77.2 %psum.29 = f32[512]{0:T(512)S(1)} all-reduce(f32[512]{0:T(512)S(1)} %reduce_sum.37), channel_id=1, replica_groups=mesh['row'=8,'col'=32] {'row','col'}, use_global_device_ids=true, to_apply=%region_4.5 | all-reduce | flops 512 | bytes 4096 | tf_op jit(solution)/shard_map/psum | solution.py:10
  214.6 0.0 copy-done.2
  214.6 0.9 fusion.14
  215.5 19.7 %all_gather.7 = bf16[512,512]{1,0:T(8,128)(2,1)S(1)} all-gather(bf16[64,512]{1,0:T(8,128)(2,1)S(1)} %fusion.14), channel_id=1, replica_groups=mesh['row'=8,'col'=32] {'row'}, dimensions={0}, use_global_device_ids=true | all-gather | bytes 589824 | tf_op jit(solution)/shard_map/all_gather | solution.py:27
  235.2 0.0 copy-done
  235.2 3.3 multiply_bitcast_fusion
  238.5 5.3 %copy.20 = f32[2048,512]{1,0:T(8,128)} copy(f32[2048,512]{0,1:T(8,128)} %multiply_bitcast_fusion) | data formatting | bytes 8388608
  243.9 0.0 reduce-scatter.9.cloned.1.call-update
  243.9 4.5 %fusion.20 = (bf16[1,2048,512]{2,1,0:T(8,128)(2,1)}, bf16[1,2048,512]{2,1,0:T(8,128)(2,1)}) fusion(bf16[2,2048,512]{2,1,0:T(8,128)(2,1)} %param.6), kind=kLoop, calls=%fused_computation.35 | loop fusion | bytes 8388608 | tf_op jit(solution)/shard_map/slice | solution.py:28
  248.4 0.0 copy-start.1
  248.4 3.0 copy.24
  251.4 3.9 copy.25
  255.3 0.0 copy-done.1
  255.3 0.1 copy.19
  255.4 0.2 fusion.12
  255.7 77.9 %reduce-scatter.9.cloned.1.call-done = f32[64,512]{1,0:T(8,128)} async-done(((f32[2048,512]{1,0:T(8,128)}), f32[64,512]{1,0:T(8,128)}) %reduce-scatter.9.cloned.1.call-update) | async-done | bytes 131088
  333.6 1.0 copy.21
  334.6 1.1 fusion.11
  335.8 0.9 reduce_sum.39
  336.7 77.3 %all-reduce = (f32[512]{0:T(512)S(1)}, f32[512]{0:T(512)S(1)}, f32[512]{0:T(512)S(1)}) all-reduce(f32[512]{0:T(512)S(1)} %fusion.11, f32[512]{0:T(512)S(1)} %fusion.12, f32[512]{0:T(512)S(1)} %reduce_sum.39), channel_id=1, replica_groups=mesh['row'=8,'col'=32] {'row','col'}, use_global_device_ids=true, to_apply=%region_7.8 | all-reduce | flops 1536 | bytes 12288 | tf_op jit(solution)/shard_map/psum | solution.py:10
  414.0 3.8 fusion.4
  417.7 2.0 fusion.5
  419.8 0.1 broadcast_divide_fusion
  419.9 0.8 copy.17
  420.7 7.3 %multiply_multiply_fusion = f32[2048,512]{1,0:T(8,128)} fusion(bf16[2048,512]{1,0:T(8,128)(2,1)} %param.5, bf16[2048,512]{0,1:T(8,128)(2,1)} %fusion.4, bf16[2048,512]{0,1:T(8,128)(2,1)} %fusion.5, bf16[512,512]{1,0:T(8,128)(2,1)S(1)} %all_gather.7, bf16[512,512]{1,0:T(8,128)(2,1)S(1)} %all_gather.6), kind=kOutput, calls=%fused_computation.8 | convolution fusion | flops 2161115136 | bytes 11534336 | tf_op jit(solution)/shard_map/dot_general | solution.py:45
  428.0 0.6 pad_maximum_fusion
  (3 shorter events, 0.0 us)
Async XLA Ops:
  7.2 129.2 %reduce-scatter.7.cloned.1.call-start = ((), (), s32[]{:S(2)}) async-start(), calls=%async_computation.2 | async-start | bytes 4325376 | tf_op jit(solution)/shard_map/reduce_scatter | solution.py:30
  42.9 171.7 %copy-start.2 = (bf16[2,64,512]{2,1,0:T(8,128)(2,1)S(1)}, bf16[2,64,512]{2,1,0:T(8,128)(2,1)}, u32[]{:S(2)}) copy-start(bf16[2,64,512]{2,1,0:T(8,128)(2,1)} %param.7) | copy-start | bytes 393220
  42.9 192.3 %copy-start = (bf16[2048,512]{1,0:T(8,128)(2,1)S(1)}, bf16[2048,512]{1,0:T(8,128)(2,1)}, u32[]{:S(2)}) copy-start(bf16[2048,512]{1,0:T(8,128)(2,1)} %param.5) | copy-start | bytes 6291460
  43.0 290.6 %reduce-scatter.9.cloned.1.call-start = ((), (), s32[]{:S(2)}) async-start(), calls=%async_computation.3 | async-start | bytes 4325376
  248.4 6.9 %copy-start.1 = (f32[64,512]{1,0:T(8,128)S(1)}, f32[64,512]{1,0:T(8,128)}, u32[]{:S(2)}) copy-start(f32[64,512]{1,0:T(8,128)} %reduce-scatter.7.cloned.1.call-done) | copy-start | bytes 393220
Sparse Core Ops, SparseCore 0:
  43.1 93.2 reduce-scatter.6
  244.0 89.5 reduce-scatter.8
where the time goes:
time: 436 us; the launch traced here: 435 us
  blocking collectives  198 us (45%)
  waiting for transfers between devices  171 us (39%)
  local copies, waits for them, and re-layouts  24 us (6%)
  matrix products  15.6 us (4%)
  between operations  14.1 us (3%)
  other arithmetic  12.4 us (3%)
    psum x2, blocking collectives, global_totals(): return lax.psum((weighted, plain), ('row', 'col'))  155 us
    reduce_scatter x1, waiting for transfers between devices, local(): lax.psum_scatter(jnp.dot(transitions, weights_col, preferred_element_type...  93.4 us
    unnamed x3, waiting for transfers between devices  77.9 us
    all_gather x2, blocking collectives, local(): weights_col = lax.all_gather(weights, 'row', axis=0, tiled=True)  43.4 us
    unnamed x13, local copies, waits for them, and re-layouts  19.5 us
  transfers between devices with their start and end apart: 2, of which 2 were waited for; matrix products, arithmetic and copies ran while one was open for 3% of the time, Pallas kernels for 0%

commit v1 on v0

v1 whole, which is shorter than its diff:
```python
import jax
import jax.numpy as jnp
from jax import lax
from jax.sharding import Mesh, PartitionSpec as P

VOCAB = 50257
COL = ("y", "x", "core")
CHIPS = ("y", "x")
BF16 = jnp.bfloat16
F16 = jnp.float16
F32 = jnp.float32


def split3(v):
    hi = lax.reduce_precision(v, 8, 7)
    mid = lax.reduce_precision(v - hi, 8, 7)
    return [part.astype(BF16) for part in (hi, mid, v - hi - mid)]


def split2(v):
    hi = lax.reduce_precision(v, 5, 10)
    return [hi.astype(F16), (v - hi).astype(F16)]


def rows8(rows):
    block = jnp.stack(rows)
    return jnp.pad(block, ((0, 8 - block.shape[0]), (0, 0)))


def local(transitions, forward, emission, beta_end, token_ids):
    src, dst = transitions.shape
    piece, seqs = beta_end.shape
    n_row = lax.axis_size("row")
    n_chip = lax.axis_size("y") * lax.axis_size("x")
    n_core = lax.axis_size("core")
    states = float(dst * n_chip * n_core)
    core = lax.axis_index("core")
    swap = [(i, (i + 1) % n_core) for i in range(n_core)]

    def observed(step):
        ended = token_ids[step] == VOCAB - 1
        return jnp.where(ended[None, :], F32(1.0), emission[step].astype(F32))

    def gather(weights, extra):
        block = jnp.concatenate([weights, rows8(extra)], axis=0)
        block = jnp.broadcast_to(block[None], (n_row,) + block.shape)
        return lax.all_to_all(block, "row", 0, 0)

    def body(block):
        return block[:, :piece].reshape(n_row * piece, seqs)

    def extras(block, i):
        return jnp.sum(block[:, piece + i:piece + i + 3].astype(F32), axis=(0, 1))

    chunks = transitions.reshape(n_chip, n_core, piece, dst)
    half = n_chip * piece
    mine = lax.dynamic_index_in_dim(chunks, core, 1, keepdims=False).reshape(half, dst)
    theirs = lax.dynamic_index_in_dim(chunks, 1 - core, 1, keepdims=False).reshape(half, dst)
    t_other = lax.ppermute(theirs, "core", swap)
    fwd = lax.dynamic_index_in_dim(
        forward.reshape(2, n_chip, n_core, piece, seqs), core, 2, keepdims=False
    ).reshape(2, half, seqs)

    g_part = lax.dot_general(
        transitions, forward[0], (((0,), (0,)), ((), ())), preferred_element_type=F32
    )
    g_own = lax.psum_scatter(g_part, "row", scatter_dimension=0, tiled=True)

    def backward(block, other, cs_own, cs_other, norm_chip, step):
        w_own, w_other = body(block), body(other)
        sc = jnp.dot(cs_own, w_own, preferred_element_type=F32)
        sc = sc + jnp.dot(cs_other, w_other, preferred_element_type=F32)
        sc = jnp.sum(sc, axis=0) / states / states
        part = jnp.dot(mine, w_own, preferred_element_type=F32)
        part = part + jnp.dot(t_other, w_other, preferred_element_type=F32)
        part = part / states
        if norm_chip is None:
            norm_chip = jnp.sum(fwd[step].astype(F32) * part, axis=0) / states
        power = jnp.ceil(jnp.log2(sc))
        down = jnp.exp2(-power)
        data = (part * down[None, :]).astype(F16).reshape(n_chip, piece, seqs)
        extra = rows8([power.astype(F16)] + split2(sc * down) + split2(norm_chip * down))
        extra = jnp.broadcast_to(extra[None], (n_chip,) + extra.shape)
        got = lax.all_to_all(jnp.concatenate([data, extra], axis=1), CHIPS, 0, 0).astype(F32)
        up = jnp.exp2(got[:, piece:piece + 1])
        raw = jnp.sum(got[:, :piece] * up, axis=0)
        scale = jnp.sum(got[:, piece + 1:piece + 3] * up, axis=(0, 1))
        norm = jnp.sum(got[:, piece + 3:piece + 5] * up, axis=(0, 1))
        return w_own, raw, scale, norm

    weights = (observed(1) * beta_end).astype(BF16)
    colsum = jnp.sum(transitions.astype(F32), axis=0)
    block = gather(weights, split3(colsum))
    other = lax.ppermute(block, "core", swap)
    cs_own = jnp.stack(split3(extras(block, 0)))
    cs_other = jnp.stack(split3(extras(other, 0)))
    w1, raw, scale1, norm1_part = backward(block, other, cs_own, cs_other, None, 1)

    weights = (observed(0) * (raw / scale1[None, :])).astype(BF16)
    norm0_part = jnp.sum(weights.astype(F32) * g_own, axis=0) / states / states
    block = gather(weights, split3(norm1_part) + split3(norm0_part))
    other = lax.ppermute(block, "core", swap)
    norm1 = extras(block, 0) + extras(other, 0)
    norm0_chip = extras(block, 3) + extras(other, 3)
    w0, raw, scale0, norm0 = backward(block, other, cs_own, cs_other, norm0_chip, 0)
    beta = raw / scale0[None, :]

    post1 = (forward[1].astype(F32) / norm1[None, :]).astype(BF16)
    post0 = (forward[0].astype(F32) / norm0[None, :]).astype(BF16)
    mixed = lax.dot_general(post1, w1, (((1,), (1,)), ((), ())), preferred_element_type=F32)
    mixed = mixed + lax.dot_general(post0, w0, (((1,), (1,)), ((), ())), preferred_element_type=F32)
    counts = transitions.astype(F32) * mixed / seqs
    return counts, beta, jnp.stack([jnp.log(scale0), jnp.log(scale1)])


def solution(mesh):
    n_row, n_col = mesh.devices.shape
    grid = Mesh(mesh.devices.reshape(n_row, 4, n_col // 8, 2), ("row",) + COL)
    in_specs = (
        P("row", COL),
        P(None, "row", None),
        P(None, ("row",) + COL, None),
        P(("row",) + COL, None),
        P(),
    )
    out_specs = (P("row", COL), P(("row",) + COL, None), P())
    return jax.shard_map(local, mesh=grid, in_specs=in_specs, out_specs=out_specs, check_vma=False)
```

time: 436 us -> 147 us (0.34)
  blocking collectives: 198 us -> 44.6 us
  waiting for transfers between devices: 171 us -> 28.4 us
  starting transfers between devices: 0.08 us -> 17.2 us
  local copies, waits for them, and re-layouts: 24 us -> 9.45 us
  matrix products: 15.6 us -> 22.2 us
    psum x2 -> x0, blocking collectives: 155 us -> none  [global_totals(): return lax.psum((weighted, plain), ('row', 'col'))]
    reduce_scatter x1, waiting for transfers between devices: 93.4 us -> 0.02 us  [local(): g_own = lax.psum_scatter(g_part, 'row', scatter_dimension=0, tiled=True)]
    unnamed x3 -> x1, waiting for transfers between devices: 77.9 us -> 0.02 us
    all_to_all x0 -> x2, blocking collectives: none -> 44.6 us  [the longest x1 25 us: backward(): lax.all_to_all(jnp.concatenate([data, extra], axis=1), CHIPS, 0, 0)]
    all_gather x2 -> x0, blocking collectives: 43.4 us -> none  [local(): weights_col = lax.all_gather(weights, 'row', axis=0, tiled=True)]
    all_to_all x0 -> x2, waiting for transfers between devices: none -> 28.3 us  [the longest x1 16.1 us: backward(): lax.all_to_all(jnp.concatenate([data, extra], axis=1), CHIPS, 0, 0)]
    unnamed x13 -> x20, local copies, waits for them, and re-layouts: 19.5 us -> 1.93 us
    all_to_all x0 -> x2, starting transfers between devices: none -> 12.9 us  [the longest x1 9.01 us: gather(): return lax.all_to_all(block, 'row', 0, 0)]
  transfers between devices with their start and end apart: 2 -> 6, of which waited for: 2 -> 2; matrix products, arithmetic and copies ran while one was open for 3% -> 15% of each run, Pallas kernels for 0% -> 0%
where the time goes in v1:
time: 147 us; the launch traced here: 146 us
  blocking collectives  44.6 us (30%)
  waiting for transfers between devices  28.4 us (19%)
  matrix products  22.2 us (15%)
  starting transfers between devices  17.2 us (12%)
  between operations  14.4 us (10%)
  other arithmetic  9.9 us (7%)
  local copies, waits for them, and re-layouts  9.45 us (6%)
    all_to_all x1, blocking collectives, backward(): lax.all_to_all(jnp.concatenate([data, extra], axis=1), CHIPS, 0, 0)  25 us
    all_to_all x1, blocking collectives, gather(): return lax.all_to_all(block, 'row', 0, 0)  19.6 us
    all_to_all x1, waiting for transfers between devices, backward(): lax.all_to_all(jnp.concatenate([data, extra], axis=1), CHIPS, 0, 0)  16.1 us
    all_to_all x1, waiting for transfers between devices, gather(): return lax.all_to_all(block, 'row', 0, 0)  12.3 us
    all_to_all x1, starting transfers between devices, gather(): return lax.all_to_all(block, 'row', 0, 0)  9.01 us
    dot_general x2, matrix products, backward(): part = part + jnp.dot(t_other, w_other, preferred_element_type=F32)  5.81 us
    dot_general x1, matrix products, local(): lax.dot_general(post0, w0, (((1,), (1,)), ((), ())), preferred_element_ty...  5.68 us
    dot_general x1, matrix products, local(): lax.dot_general(post1, w1, (((1,), (1,)), ((), ())), preferred_element_ty...  4.98 us
  transfers between devices with their start and end apart: 6, of which 2 were waited for; matrix products, arithmetic and copies ran while one was open for 15% of the time, Pallas kernels for 0%

profile of v1, /device:TPU:1, one launch (start us, length us, event | category | flops | bytes accessed | tf_op | source)
XLA Modules:
  0.0 146.1 jit_solution(4474193989847548169)
XLA Ops:
  7.2 0.0 copy-start
  7.2 0.0 copy-start.8
  7.2 2.1 %convert_reduce_fusion = f32[512]{0:T(512)S(1)} fusion(bf16[2048,512]{1,0:T(8,128)(2,1)} %param.5), kind=kLoop, calls=%fused_computation.1 | loop fusion | flops 2096640 | bytes 2099200 | tf_op jit(solution)/shard_map/reduce_sum | solution.py:92
  9.3 0.0 copy-done.8
  9.3 0.9 fusion.20
  10.3 0.8 broadcast_in_dim.59
  11.1 9.0 %all-to-all-start = ((bf16[8,72,512]{2,1,0:T(8,128)(2,1)}), bf16[8,72,512]{2,1,0:T(8,128)(2,1)}, u32[]{:S(2)}, u32[]{:S(2)}) async-start(bf16[8,72,512]{2,1,0:T(8,128)(2,1)} %broadcast_in_dim.59), calls=%async_computation | async-start | bytes 1179648 | tf_op jit(solution)/shard_map/all_to_all | solution.py:47
  20.1 0.0 reduce-scatter.2.cloned.1.call-start
  20.2 0.0 copy-done
  20.2 0.0 copy-start.5
  20.2 1.2 constant_dynamic-slice_fusion.1
  21.5 1.0 collective-permute-start
  22.4 0.4 copy-done.5
  22.8 2.3 %fusion.9 = f32[512,512]{1,0:T(8,128)} fusion(bf16[2048,512]{1,0:T(8,128)(2,1)S(1)} %copy-done, bf16[2,2048,512]{2,1,0:T(8,128)(2,1)S(1)} %copy-done.5), kind=kOutput, calls=%fused_computation.14 | convolution fusion | flops 1073741824 | bytes 5242880 | tf_op jit(solution)/shard_map/dot_general | solution.py:64
  25.0 0.0 reduce-scatter.2.cloned.1.call-update
  25.1 2.3 %constant_dynamic-slice_fusion = bf16[1,16,1,64,512]{4,3,2,1,0:T(8,128)(2,1)} fusion(bf16[2,16,2,64,512]{4,3,2,1,0:T(8,128)(2,1)} %bitcast.79, s32[]{:T(128)S(6)} %add.71, s32[]{:T(128)S(6)} %select_n.17), kind=kLoop, calls=%fused_computation.120 | loop fusion | bytes 2097160 | tf_op jit(solution)/shard_map/slice | solution.py:78
  27.4 12.3 %all-to-all-done = bf16[8,72,512]{2,1,0:T(8,128)(2,1)} async-done(((bf16[8,72,512]{2,1,0:T(8,128)(2,1)}), bf16[8,72,512]{2,1,0:T(8,128)(2,1)}, u32[]{:S(2)}, u32[]{:S(2)}) %all-to-all-start) | async-done | bytes 589856 | tf_op jit(solution)/shard_map/all_to_all | solution.py:47
  39.6 1.2 copy.22
  40.9 0.6 collective-permute-start.1
  41.5 1.1 slice.102
  42.6 0.0 copy-start.1
  42.6 0.2 fusion.47
  42.7 0.7 fusion.49
  43.5 0.0 copy-done.1
  43.5 0.0 copy-start.4
  43.5 0.0 collective-permute-done.1
  43.5 0.2 copy.23
  43.7 0.2 fusion.16
  43.9 0.0 collective-permute-done
  44.0 0.7 copy-done.4
  44.7 3.2 %multiply_convert_fusion.1 = (f16[1024,512]{1,0:T(8,128)(2,1)}, f32[512]{0:T(512)S(1)}) fusion(f32[512]{0:T(512)S(1)} %get-tuple-element.37, bf16[1,16,1,64,512]{4,3,2,1,0:T(8,128)(2,1)S(1)} %copy-done.4, f32[1024,512]{1,0:T(8,128)S(1)} %fusion.49, bf16[1024,512]{1,0:T(8,128)(2,1)} %collective-permute-done, bf16[512,512]{1,0:T(8,128)(2,1)S(1)} %bitcast.76), kind=kOutput, calls=%fused_computation.19 | convolution fusion | flops 540540416 | bytes 5771264 | tf_op jit(solution)/shard_map/dot_general | solution.py:75
  48.0 1.5 %pad_maximum_fusion = f16[16,72,512]{2,1,0:T(8,128)(2,1)S(1)} fusion(f16[16,8,512]{2,1,0:T(8,128)(2,1)S(1)} %broadcast_in_dim.60, f16[16,64,512]{2,1,0:T(8,128)(2,1)} %bitcast.77), kind=kLoop, calls=%fused_computation.24 | loop fusion | flops 589824 | bytes 2359296 | tf_op jit(solution)/shard_map/concatenate | solution.py:84
  49.6 25.0 %all_to_all.20 = f16[16,72,512]{2,1,0:T(8,128)(2,1)S(1)} all-to-all(f16[16,72,512]{2,1,0:T(8,128)(2,1)S(1)} %pad_maximum_fusion), channel_id=1, replica_groups=mesh['row'=8,'y'=4,'x'=4,'core'=2] {'y','x'}, dimensions={0} | all-to-all | bytes 2359296 | tf_op jit(solution)/shard_map/all_to_all | solution.py:84
  74.5 0.3 convert_element_type.364
  74.9 0.0 copy-start.7
  74.9 0.1 fusion.27
  75.0 0.3 fusion.7
  75.3 0.0 reduce-scatter.2.cloned.1.call-done
  75.3 0.4 copy-done.7
  75.8 1.0 multiply_reduce_fusion
  76.9 19.6 %all_to_all.21 = bf16[8,72,512]{2,1,0:T(8,128)(2,1)S(1)} all-to-all(bf16[8,72,512]{2,1,0:T(8,128)(2,1)S(1)} %broadcast_in_dim.61), channel_id=1, replica_groups=mesh['row'=8,'y'=4,'x'=4,'core'=2] {'row'}, dimensions={0} | all-to-all | bytes 1179648 | tf_op jit(solution)/shard_map/all_to_all | solution.py:47
  96.4 0.2 copy.26
  96.6 2.7 %collective-permute-start.2 = (bf16[8,72,512]{2,0,1:T(8,128)(2,1)S(1)}, bf16[8,72,512]{2,0,1:T(8,128)(2,1)S(1)}, u32[]{:S(2)}, u32[]{:S(2)}) collective-permute-start(bf16[8,72,512]{2,0,1:T(8,128)(2,1)S(1)} %copy.26), channel_id=1, source_target_pairs={{0,1},{1,0},{2,3},{3,2},{4,5},{5,4},{6,7},{7,6},{8,9},{9,8},{10,11... | collective-permute-start | bytes 1769480 | tf_op jit(solution)/shard_map/ppermute | solution.py:102
  99.4 0.0 copy-start.2
  99.4 0.2 fusion.46
  99.6 2.0 %fusion.50 = f32[1024,512]{1,0:T(8,128)} fusion(bf16[1024,512]{1,0:T(8,128)(2,1)S(1)} %bitcast.66, bf16[512,512]{1,0:T(8,128)(2,1)S(1)} %bitcast.71), kind=kOutput, calls=%fused_computation.128 | convolution fusion | flops 536870912 | bytes 3670016 | tf_op jit(solution)/shard_map/dot_general | solution.py:74
  101.6 0.0 copy-done.2
  101.6 0.0 collective-permute-done.2
  101.7 0.2 copy.28
  101.8 0.2 fusion.17
  102.2 2.6 %multiply_convert_fusion = f16[1024,512]{1,0:T(8,128)(2,1)S(1)} fusion(f32[1024,512]{1,0:T(8,128)} %fusion.50, bf16[1024,512]{1,0:T(8,128)(2,1)} %collective-permute-done, bf16[512,512]{1,0:T(8,128)(2,1)S(1)} %bitcast.74, f32[512]{0:T(512)S(1)} %get-tuple-element.27), kind=kOutput, calls=%fused_computation.17 | convolution fusion | flops 538443776 | bytes 4720640 | tf_op jit(solution)/shard_map/dot_general | solution.py:75
  104.9 1.3 pad_maximum_fusion.1
  106.2 3.9 %all-to-all-start.3 = ((f16[16,72,512]{2,1,0:T(8,128)(2,1)}), f16[16,72,512]{2,1,0:T(8,128)(2,1)S(1)}, u32[]{:S(2)}, u32[]{:S(2)}) async-start(f16[16,72,512]{2,1,0:T(8,128)(2,1)} %pad_maximum_fusion.1), calls=%async_computation.4 | async-start | bytes 2359296 | tf_op jit(solution)/shard_map/all_to_all | solution.py:84
  110.1 5.0 %fusion.2 = f32[2048,512]{1,0:T(8,128)} fusion(bf16[512,512]{1,0:T(8,128)(2,1)} %bitcast.69, f32[512]{0:T(512)S(1)} %add.63, bf16[2,2048,512]{2,1,0:T(8,128)(2,1)} %param.6), kind=kOutput, calls=%fused_computation.6 | convolution fusion | flops 1076887552 | bytes 6817792 | tf_op jit(solution)/shard_map/dot_general | solution.py:110
  115.1 16.1 %all-to-all-done.3 = f16[16,72,512]{2,1,0:T(8,128)(2,1)S(1)} async-done(((f16[16,72,512]{2,1,0:T(8,128)(2,1)}), f16[16,72,512]{2,1,0:T(8,128)(2,1)S(1)}, u32[]{:S(2)}, u32[]{:S(2)}) %all-to-all-start.3) | async-done | bytes 1179680 | tf_op jit(solution)/shard_map/all_to_all | solution.py:84
  131.1 0.3 convert_element_type.386
  131.5 0.0 copy-start.3
  131.5 0.1 fusion.24
  131.7 0.3 fusion.6
  131.9 0.7 broadcast_divide_fusion
  132.6 0.6 pad_maximum_fusion.5
  133.2 0.2 copy-done.6
  133.4 0.2 copy-done.3
  133.6 5.7 %fusion = f32[2048,512]{1,0:T(8,128)} fusion(bf16[2048,512]{1,0:T(8,128)(2,1)S(1)} %copy-done, f32[2048,512]{1,0:T(8,128)} %fusion.2, bf16[512,512]{1,0:T(8,128)(2,1)S(1)} %bitcast.72, f32[512]{0:T(512)S(1)} %get-tuple-element.4, bf16[2,2048,512]{2,1,0:T(8,128)(2,1)S(1)} %copy-done.6), kind=kOutput, calls=%fused_computation.2 | convolution fusion | flops 1081081856 | bytes 13109248 | tf_op jit(solution)/shard_map/dot_general | solution.py:111
  (40 shorter events, 0.8 us)
Async XLA Ops:
  7.2 13.0 %copy-start = (bf16[2048,512]{1,0:T(8,128)(2,1)S(1)}, bf16[2048,512]{1,0:T(8,128)(2,1)}, u32[]{:S(2)}) copy-start(bf16[2048,512]{1,0:T(8,128)(2,1)} %param.5) | copy-start | bytes 6291460
  7.2 2.1 %copy-start.8 = (s32[2,512]{1,0:T(2,128)S(1)}, s32[2,512]{1,0:T(2,128)}, u32[]{:S(2)}) copy-start(s32[2,512]{1,0:T(2,128)} %param.9) | copy-start | bytes 12292
  11.1 28.5 %all-to-all-start = ((bf16[8,72,512]{2,1,0:T(8,128)(2,1)}), bf16[8,72,512]{2,1,0:T(8,128)(2,1)}, u32[]{:S(2)}, u32[]{:S(2)}) async-start(bf16[8,72,512]{2,1,0:T(8,128)(2,1)} %broadcast_in_dim.59), calls=%async_computation | async-start | bytes 1179648 | tf_op jit(solution)/shard_map/all_to_all | solution.py:47
  20.1 55.2 %reduce-scatter.2.cloned.1.call-start = ((), (), s32[]{:S(2)}) async-start(), calls=%async_computation.5 | async-start | bytes 1179648 | tf_op jit(solution)/shard_map/reduce_scatter | solution.py:67
  20.2 2.6 %copy-start.5 = (bf16[2,2048,512]{2,1,0:T(8,128)(2,1)S(1)}, bf16[2,2048,512]{2,1,0:T(8,128)(2,1)}, u32[]{:S(2)}) copy-start(bf16[2,2048,512]{2,1,0:T(8,128)(2,1)} %param.6) | copy-start | bytes 12582916
  21.5 22.5 %collective-permute-start = (bf16[1024,512]{1,0:T(8,128)(2,1)}, bf16[1024,512]{1,0:T(8,128)(2,1)}, u32[]{:S(2)}, u32[]{:S(2)}) collective-permute-start(bf16[1024,512]{1,0:T(8,128)(2,1)} %bitcast.6), channel_id=1, source_target_pairs={{0,1},{1,0},{2,3},{3,2},{4,5},{5,4},{6,7},{7,6},{8,9},{9,8},{10,11... | collective-permute-start | bytes 3145736 | tf_op jit(solution)/shard_map/ppermute | solution.py:59
  40.9 2.6 %collective-permute-start.1 = (bf16[8,72,512]{2,0,1:T(8,128)(2,1)S(1)}, bf16[8,72,512]{2,0,1:T(8,128)(2,1)S(1)}, u32[]{:S(2)}, u32[]{:S(2)}) collective-permute-start(bf16[8,72,512]{2,0,1:T(8,128)(2,1)S(1)} %copy.22), channel_id=1, source_target_pairs={{0,1},{1,0},{2,3},{3,2},{4,5},{5,4},{6,7},{7,6},{8,9},{9,8},{10,11... | collective-permute-start | bytes 1769480 | tf_op jit(solution)/shard_map/ppermute | solution.py:94
  42.6 0.9 copy-start.1
  43.5 1.2 copy-start.4
  74.9 0.9 copy-start.7
  96.6 5.0 %collective-permute-start.2 = (bf16[8,72,512]{2,0,1:T(8,128)(2,1)S(1)}, bf16[8,72,512]{2,0,1:T(8,128)(2,1)S(1)}, u32[]{:S(2)}, u32[]{:S(2)}) collective-permute-start(bf16[8,72,512]{2,0,1:T(8,128)(2,1)S(1)} %copy.26), channel_id=1, source_target_pairs={{0,1},{1,0},{2,3},{3,2},{4,5},{5,4},{6,7},{7,6},{8,9},{9,8},{10,11... | collective-permute-start | bytes 1769480 | tf_op jit(solution)/shard_map/ppermute | solution.py:102
  99.4 2.2 %copy-start.2 = (bf16[8,64,512]{2,1,0:T(8,128)(2,1)}, bf16[8,64,512]{2,1,0:T(8,128)(2,1)S(1)}, u32[]{:S(2)}) copy-start(bf16[8,64,512]{2,1,0:T(8,128)(2,1)S(1)} %slice.112) | copy-start | bytes 1572868
  106.2 24.9 %all-to-all-start.3 = ((f16[16,72,512]{2,1,0:T(8,128)(2,1)}), f16[16,72,512]{2,1,0:T(8,128)(2,1)S(1)}, u32[]{:S(2)}, u32[]{:S(2)}) async-start(f16[16,72,512]{2,1,0:T(8,128)(2,1)} %pad_maximum_fusion.1), calls=%async_computation.4 | async-start | bytes 2359296 | tf_op jit(solution)/shard_map/all_to_all | solution.py:84
  131.1 2.2 %copy-start.6 = (bf16[2,2048,512]{2,1,0:T(8,128)(2,1)S(1)}, bf16[2,2048,512]{2,1,0:T(8,128)(2,1)}, u32[]{:S(2)}) copy-start(bf16[2,2048,512]{2,1,0:T(8,128)(2,1)} %param.6) | copy-start | bytes 12582916
  131.5 2.1 %copy-start.3 = (bf16[8,64,512]{2,1,0:T(8,128)(2,1)S(1)}, bf16[8,64,512]{2,1,0:T(8,128)(2,1)}, u32[]{:S(2)}) copy-start(bf16[8,64,512]{2,1,0:T(8,128)(2,1)} %copy-done.2) | copy-start | bytes 1572868
Sparse Core Ops, SparseCore 0:
  25.2 35.6 reduce-scatter.1

commit v2 on v1

v2 whole, which is shorter than its diff:
```python
import jax
import jax.numpy as jnp
from jax import lax
from jax.experimental import pallas as pl
from jax.experimental.pallas import tpu as pltpu
from jax.sharding import Mesh, PartitionSpec as P

VOCAB = 50257
COL = ("y", "x", "core")
CHIPS = ("y", "x")
BF16 = jnp.bfloat16
F16 = jnp.float16
F32 = jnp.float32
EXTRA = 8
TILE = 256
CHUNK = 512
NT = (((1,), (1,)), ((), ()))
TN = (((0,), (0,)), ((), ()))
WHOLE = pl.BlockSpec(memory_space=pltpu.VMEM)


def params(mib):
    return pltpu.CompilerParams(vmem_limit_bytes=mib * 1024 * 1024)


def split3(v):
    hi = lax.reduce_precision(v, 8, 7)
    mid = lax.reduce_precision(v - hi, 8, 7)
    return [part.astype(BF16) for part in (hi, mid, v - hi - mid)]


def split2(v):
    hi = lax.reduce_precision(v, 5, 10)
    return [hi, lax.reduce_precision(v - hi, 5, 10)]


def rows8(rows):
    block = jnp.stack(rows)
    return jnp.pad(block, ((0, EXTRA - block.shape[0]), (0, 0)))


def start_kernel(at_ref, t_hbm, f_hbm, e_hbm, b_hbm, tok_hbm, pay_ref, mine_ref, alpha_ref, seen_ref,
                 t_ref, f_ref, a_ref, e_ref, b_ref, tok_ref, g_ref, sems):
    core, col = at_ref[0], at_ref[1]
    piece = b_ref.shape[0]
    src = t_ref.shape[0]
    parts = src // CHUNK

    def copy(source, target, i):
        c = pltpu.make_async_copy(source, target, sems.at[i])
        c.start()
        return c

    loads = []
    for i in range(parts):
        rows = pl.ds(i * CHUNK, CHUNK)
        loads.append((
            copy(t_hbm.at[rows, :], t_ref.at[rows, :], 2 * i),
            copy(f_hbm.at[0, rows, :], f_ref.at[rows, :], 2 * i + 1),
        ))
    own = pl.ds(pl.multiple_of(col * piece, piece), piece)
    small = [
        copy(f_hbm.at[1, own, :], a_ref, 2 * parts),
        copy(e_hbm, e_ref, 2 * parts + 1),
        copy(b_hbm, b_ref, 2 * parts + 2),
        copy(tok_hbm, tok_ref, 2 * parts + 3),
    ]
    ones = jnp.ones((EXTRA, CHUNK), BF16)
    sums = jnp.zeros((EXTRA, t_ref.shape[1]), F32)
    for i in range(parts):
        for c in loads[i]:
            c.wait()
        t = t_ref[i * CHUNK:(i + 1) * CHUNK, :]
        f = f_ref[i * CHUNK:(i + 1) * CHUNK, :]
        g = lax.dot_general(t, f, TN, preferred_element_type=F32)
        if i == 0:
            g_ref[...] = g
        else:
            g_ref[...] += g
        sums = sums + jnp.dot(ones, t, preferred_element_type=F32)
    for i in range(src // (2 * piece)):
        rows = pl.ds(pl.multiple_of((2 * i + core) * piece, piece), piece)
        mine_ref[i * piece:(i + 1) * piece, :] = t_ref[rows, :]
    for c in small:
        c.wait()
    alpha_ref[...] = a_ref[...].astype(F32)
    ended = tok_ref[...] == VOCAB - 1
    seen_ref[...] = jnp.where(ended[0:1], F32(1.0), e_ref[0].astype(F32))
    observed = jnp.where(ended[1:2], F32(1.0), e_ref[1].astype(F32))
    weights = (observed * b_ref[...]).astype(BF16)
    hi = sums.astype(BF16).astype(F32)
    mid = (sums - hi).astype(BF16).astype(F32)
    lo = sums - hi - mid
    row = lax.broadcasted_iota(jnp.int32, sums.shape, 0)
    tail = jnp.where(row == 0, hi, jnp.where(row == 1, mid, jnp.where(row == 2, lo, F32(0.0))))
    tail = tail.astype(BF16)
    for r in range(pay_ref.shape[0]):
        part = g_ref[r * piece:(r + 1) * piece, :].astype(BF16)
        pay_ref[r] = jnp.concatenate([weights, part, tail], axis=0)


def start_call(at, transitions, forward, emission, beta_end, token_ids, n_row):
    src, dst = transitions.shape
    piece, seqs = beta_end.shape
    return pl.pallas_call(
        start_kernel,
        out_shape=(
            jax.ShapeDtypeStruct((n_row, 2 * piece + EXTRA, seqs), BF16),
            jax.ShapeDtypeStruct((src // 2, dst), BF16),
            jax.ShapeDtypeStruct((piece, seqs), F32),
            jax.ShapeDtypeStruct((piece, seqs), F32),
        ),
        in_specs=[pl.BlockSpec(memory_space=pltpu.SMEM)] + [pl.BlockSpec(memory_space=pl.ANY)] * 5,
        out_specs=(WHOLE,) * 4,
        scratch_shapes=[
            pltpu.VMEM((src, dst), BF16),
            pltpu.VMEM((src, seqs), BF16),
            pltpu.VMEM((piece, seqs), BF16),
            pltpu.VMEM(emission.shape, BF16),
            pltpu.VMEM((piece, seqs), F32),
            pltpu.VMEM(token_ids.shape, jnp.int32),
            pltpu.VMEM((dst, seqs), F32),
            pltpu.SemaphoreType.DMA((2 * (src // CHUNK) + 4,)),
        ],
        compiler_params=params(56),
    )(at, transitions, forward, emission, beta_end, token_ids)


def product_kernel(mine_ref, other_ref, w_ref, v_ref, mul_ref, extra_ref, out_ref):
    n_chip, rows, _ = out_ref.shape
    piece = rows - EXTRA
    mul = mul_ref[...]
    extra = extra_ref[...]
    group = TILE // piece
    for i in range(n_chip // group):
        at = pl.ds(i * TILE, TILE)
        part = jnp.dot(mine_ref[at, :], w_ref[...], preferred_element_type=F32)
        part = part + jnp.dot(other_ref[at, :], v_ref[...], preferred_element_type=F32)
        part = part * mul
        for j in range(group):
            out_ref[i * group + j, :piece, :] = part[j * piece:(j + 1) * piece]
            out_ref[i * group + j, piece:, :] = extra


def counts_kernel(t_hbm, f_hbm, w1_ref, w0_ref, raw_ref, sums_ref, out_hbm, beta_ref, log_ref,
                  t_ref, f_ref, o_ref, w1t_ref, w0t_ref, sems):
    src, seqs = f_ref.shape[1:]
    parts = src // TILE
    loads, stores = [], []
    for i in range(parts):
        rows = pl.ds(i * TILE, TILE)
        loads.append((
            pltpu.make_async_copy(t_hbm.at[rows, :], t_ref.at[rows, :], sems.at[3 * i]),
            pltpu.make_async_copy(f_hbm.at[:, rows, :], f_ref.at[:, rows, :], sems.at[3 * i + 1]),
        ))
        stores.append(pltpu.make_async_copy(o_ref.at[rows, :], out_hbm.at[rows, :], sems.at[3 * i + 2]))
        for c in loads[i]:
            c.start()
    w1t_ref[...] = w1_ref[...].T
    w0t_ref[...] = w0_ref[...].T
    beta_ref[...] = raw_ref[...] / sums_ref[2:3, :]
    log_ref[...] = jnp.log(sums_ref[2:4, :])
    inv = 1.0 / sums_ref[0:2, :]
    for i in range(parts):
        for c in loads[i]:
            c.wait()
        at = slice(i * TILE, (i + 1) * TILE)
        post1 = (f_ref[1, at, :].astype(F32) * inv[1:2]).astype(BF16)
        post0 = (f_ref[0, at, :].astype(F32) * inv[0:1]).astype(BF16)
        mixed = jnp.dot(post1, w1t_ref[...], preferred_element_type=F32)
        mixed = mixed + jnp.dot(post0, w0t_ref[...], preferred_element_type=F32)
        o_ref[at, :] = t_ref[at, :].astype(F32) * (mixed * (1.0 / seqs))
        stores[i].start()
    for c in stores:
        c.wait()


def counts_call(transitions, forward, w1, w0, raw, sums):
    src, dst = transitions.shape
    steps, _, seqs = forward.shape
    return pl.pallas_call(
        counts_kernel,
        out_shape=(
            jax.ShapeDtypeStruct((src, dst), F32),
            jax.ShapeDtypeStruct(raw.shape, F32),
            jax.ShapeDtypeStruct((steps, seqs), F32),
        ),
        in_specs=[pl.BlockSpec(memory_space=pl.ANY)] * 2 + [WHOLE] * 4,
        out_specs=(pl.BlockSpec(memory_space=pl.ANY), WHOLE, WHOLE),
        scratch_shapes=[
            pltpu.VMEM((src, dst), BF16),
            pltpu.VMEM((steps, src, seqs), BF16),
            pltpu.VMEM((src, dst), F32),
            pltpu.VMEM((seqs, dst), BF16),
            pltpu.VMEM((seqs, dst), BF16),
            pltpu.SemaphoreType.DMA((3 * (src // TILE),)),
        ],
        compiler_params=params(56),
    )(transitions, forward, w1, w0, raw, sums)


def local(transitions, forward, emission, beta_end, token_ids):
    src, dst = transitions.shape
    piece, seqs = beta_end.shape
    n_row = lax.axis_size("row")
    n_chip = lax.axis_size("y") * lax.axis_size("x")
    n_core = lax.axis_size("core")
    states = float(dst * n_chip * n_core)
    core = lax.axis_index("core")
    col = (lax.axis_index("y") * lax.axis_size("x") + lax.axis_index("x")) * n_core + core
    swap = [(i, (i + 1) % n_core) for i in range(n_core)]

    chunks = transitions.reshape(n_chip, n_core, piece, dst)
    theirs = lax.dynamic_index_in_dim(chunks, 1 - core, 1, keepdims=False).reshape(src // 2, dst)
    t_other = lax.ppermute(theirs, "core", swap)
    at = jnp.stack([core, col]).astype(jnp.int32)
    pay, mine, alpha, observed = start_call(
        at, transitions, forward, emission, beta_end, token_ids, n_row
    )
    pay, mine, t_other = lax.optimization_barrier((pay, mine, t_other))

    block = lax.all_to_all(pay, "row", 0, 0)
    w1 = block[:, :piece].reshape(dst, seqs)
    g_own = jnp.sum(block[:, piece:2 * piece].astype(F32), axis=0)
    cs = jnp.sum(block[:, 2 * piece:2 * piece + 3].astype(F32), axis=(0, 1))
    cs = jnp.stack(split3(cs))

    def backward(w_own, totals):
        w_other = lax.ppermute(w_own, "core", swap)
        sc = jnp.sum(jnp.dot(cs, w_own, preferred_element_type=F32), axis=0) / states / states
        own = jnp.stack([sc] + totals)
        both = own + lax.ppermute(own, "core", swap)
        power = jnp.ceil(jnp.log2(both[0]))
        down = jnp.exp2(-power)
        rows = [power]
        for i in range(both.shape[0]):
            rows += split2(both[i] * down)
        data = pl.pallas_call(
            product_kernel,
            out_shape=jax.ShapeDtypeStruct((n_chip, piece + EXTRA, seqs), F32),
            in_specs=[WHOLE] * 6,
            out_specs=WHOLE,
            compiler_params=params(16),
        )(mine, t_other, w_own, w_other, (down / states)[None, :], rows8(rows))
        return data.astype(F16), both.shape[0]

    def collect(data, n):
        got = lax.all_to_all(data, CHIPS, 0, 0).astype(F32)
        up = jnp.exp2(got[:, piece:piece + 1])
        raw = jnp.sum(got[:, :piece] * up, axis=0)
        sums = jnp.sum(got[:, piece + 1:] * up, axis=0)
        return raw, [sums[2 * i] + sums[2 * i + 1] for i in range(n)]

    data, n = backward(w1, [])
    data, g_own = lax.optimization_barrier((data, g_own))
    raw, (scale1,) = collect(data, n)

    weights = (observed * (raw / scale1[None, :])).astype(BF16)
    norm1 = jnp.sum(alpha * raw, axis=0) / states
    norm0 = jnp.sum(weights.astype(F32) * g_own, axis=0) / states / states
    pay = jnp.concatenate([weights, rows8(split3(norm1) + split3(norm0))], axis=0)
    block = lax.all_to_all(jnp.broadcast_to(pay[None], (n_row,) + pay.shape), "row", 0, 0)
    w0 = block[:, :piece].reshape(dst, seqs)
    sums = jnp.sum(block[:, piece:].astype(F32), axis=0)
    norm1 = sums[0] + sums[1] + sums[2]
    norm0 = sums[3] + sums[4] + sums[5]
    data, n = backward(w0, [norm1, norm0])
    raw, (scale0, norm1, norm0) = collect(data, n)

    sums = rows8([norm0, norm1, scale0, scale1])
    return counts_call(transitions, forward, w1, w0, raw, sums)


def solution(mesh):
    n_row, n_col = mesh.devices.shape
    grid = Mesh(mesh.devices.reshape(n_row, 4, n_col // 8, 2), ("row",) + COL)
    in_specs = (
        P("row", COL),
        P(None, "row", None),
        P(None, ("row",) + COL, None),
        P(("row",) + COL, None),
        P(),
    )
    out_specs = (P("row", COL), P(("row",) + COL, None), P())
    return jax.shard_map(local, mesh=grid, in_specs=in_specs, out_specs=out_specs, check_vma=False)
```

time: 147 us -> 136 us (0.925)
  blocking collectives: 44.6 us -> 103 us
  waiting for transfers between devices: 28.4 us -> 2.77 us
  matrix products: 22.2 us -> 0.37 us
  Pallas kernels: 0 us -> 15.2 us
  between operations: 14.4 us -> 0.98 us
  starting transfers between devices: 17.2 us -> 7.12 us
  local copies, waits for them, and re-layouts: 9.45 us -> 2.09 us
  other arithmetic: 9.9 us -> 4.36 us
    all_to_all x2 -> x4, blocking collectives: 44.6 us -> 103 us  [the longest x2 46 us: collect(): got = lax.all_to_all(data, CHIPS, 0, 0).astype(F32)]
    all_to_all x2 -> x0, waiting for transfers between devices: 28.3 us -> none  [the longest x1 16.1 us: backward(): lax.all_to_all(jnp.concatenate([data, extra], axis=1), CHIPS, 0, 0)]
    dot_general x11 -> x2, matrix products: 22.2 us -> 0.37 us  [backward(): jnp.dot(cs, w_own, preferred_element_type=F32)]
    pallas_call x0 -> x4, Pallas kernels: none -> 15.2 us  [the longest x1 7.58 us: counts_call(): pl.pallas_call(counts_kernel, out_shape=(jax.ShapeDtypeStruct((src, dst),...]
    all_to_all x2 -> x0, starting transfers between devices: 12.9 us -> none  [the longest x1 9.01 us: gather(): return lax.all_to_all(block, 'row', 0, 0)]
    slice x7 -> x2, local copies, waits for them, and re-layouts: 3.81 us -> 0.07 us  [the longest x1 0.04 us: local(): w1 = block[:, :piece].reshape(dst, seqs)]
    concatenate x4 -> x1, other arithmetic: 2.83 us -> 0.01 us  [local(): jnp.concatenate([weights, rows8(split3(norm1) + split3(norm0))], axis=0)]
    ppermute x2 -> x4, waiting for transfers between devices: 0.01 us -> 2.77 us  [the longest x2 1.86 us: backward(): both = own + lax.ppermute(own, 'core', swap)]
  transfers between devices with their start and end apart: 6 -> 5, of which waited for: 2 -> 3; matrix products, arithmetic and copies ran while one was open for 15% -> 1% of each run, Pallas kernels for 0% -> 4%
where the time goes in v2:
time: 136 us; the launch traced here: 135 us
  blocking collectives  103 us (76%)
  Pallas kernels  15.2 us (11%)
  starting transfers between devices  7.12 us (5%)
  other arithmetic  4.36 us (3%)
  waiting for transfers between devices  2.77 us (2%)
  local copies, waits for them, and re-layouts  2.09 us (2%)
    all_to_all x2, blocking collectives, collect(): got = lax.all_to_all(data, CHIPS, 0, 0).astype(F32)  46 us
    all_to_all x1, blocking collectives, local(): block = lax.all_to_all(pay, 'row', 0, 0)  37.2 us
    all_to_all x1, blocking collectives, local(): lax.all_to_all(jnp.broadcast_to(pay[None], (n_row,) + pay.shape), 'row',...  19.3 us
    pallas_call x1, Pallas kernels, counts_call(): pl.pallas_call(counts_kernel, out_shape=(jax.ShapeDtypeStruct((src, dst),...  7.58 us
    pallas_call x1, Pallas kernels, start_call(): pl.pallas_call(start_kernel, out_shape=(jax.ShapeDtypeStruct((n_row, 2 *...  5.17 us
    ppermute x1, starting transfers between devices, local(): t_other = lax.ppermute(theirs, 'core', swap)  3.33 us
    ppermute x2, starting transfers between devices, backward(): both = own + lax.ppermute(own, 'core', swap)  3.14 us
  transfers between devices with their start and end apart: 5, of which 3 were waited for; matrix products, arithmetic and copies ran while one was open for 1% of the time, Pallas kernels for 4%

profile of v2, /device:TPU:1, one launch (start us, length us, event | category | flops | bytes accessed | tf_op | source)
XLA Modules:
  0.0 135.5 jit_solution(16835845614616630939)
XLA Ops:
  0.6 1.3 constant_dynamic-slice_fusion
  2.0 3.3 %collective-permute-start = (bf16[1024,512]{1,0:T(8,128)(2,1)S(1)}, bf16[1024,512]{1,0:T(8,128)(2,1)S(1)}, u32[]{:S(2)}, u32[]{:S(2)}) collective-permute-start(bf16[1024,512]{1,0:T(8,128)(2,1)S(1)} %bitcast.31), channel_id=1, source_target_pairs={{0,1},{1,0},{2,3},{3,2},{4,5},{5,4},{6,7},{7,6},{8,9},{9,8},{10,11... | collective-permute-start | bytes 3145736 | tf_op jit(solution)/shard_map/ppermute | solution.py:215
  5.3 0.7 pad_add_fusion.at_ref
  6.0 5.2 %shard_map.76 = (bf16[8,136,512]{2,1,0:T(8,128)(2,1)}, bf16[1024,512]{1,0:T(8,128)(2,1)}, f32[64,512]{1,0:T(8,128)}, f32[64,512]{1,0:T(8,128)}) custom-call(s32[2]{0:T(128)} %pad_add_fusion.at_ref, bf16[2048,512]{1,0:T(8,128)(2,1)} %t_hbm.3, bf16[2,2048,512]{2,1,0:T(8,128)(2,1)} %f_hbm.3, bf16[2,64,512]{2,1,0:T(8,128)(2,1)} %e_hbm.1, f32[64,512]{1,0:T(8,128)} %b_hbm.1, ...), custom_call_target="tpu_custom_call" | custom-call | tf_op jit(solution)/shard_map/pallas_call | solution.py:105
  11.1 0.0 collective-permute-done.other_ref
  11.1 0.0 copy-start.2
  11.2 37.2 %all_to_all.20 = bf16[8,136,512]{2,1,0:T(8,128)(2,1)S(1)} all-to-all(bf16[8,136,512]{2,1,0:T(8,128)(2,1)} %get-tuple-element.14), channel_id=1, replica_groups=mesh['row'=8,'y'=4,'x'=4,'core'=2] {'row'}, dimensions={0} | all-to-all | bytes 2228224 | tf_op jit(solution)/shard_map/all_to_all | solution.py:222
  48.5 0.0 copy-start
  48.5 0.6 collective-permute-start.1
  49.0 0.2 convolution_reduce_fusion.1
  49.2 0.1 collective-permute-start.2
  49.4 0.1 convert_reduce_fusion
  49.4 1.1 collective-permute-done.2
  50.7 0.0 collective-permute-done.1.v_ref
  50.7 0.0 copy-done.2
  50.7 1.2 shard_map.77
  51.9 0.0 copy-done
  51.9 0.3 convert_element_type.129
  52.2 24.6 %all_to_all.21 = f16[16,72,512]{2,1,0:T(8,128)(2,1)S(1)} all-to-all(f16[16,72,512]{2,1,0:T(8,128)(2,1)S(1)} %convert_element_type.129), channel_id=1, replica_groups=mesh['row'=8,'y'=4,'x'=4,'core'=2] {'y','x'}, dimensions={0} | all-to-all | bytes 2359296 | tf_op jit(solution)/shard_map/all_to_all | solution.py:248
  76.8 0.3 convert_element_type.131
  77.2 0.0 copy-start.3
  77.2 0.0 copy-start.4
  77.2 0.1 fusion.3
  77.3 0.3 fusion.1
  77.6 0.5 copy-done.3
  78.1 0.1 copy-done.4
  78.1 0.1 multiply_reduce_fusion
  78.3 19.3 %all_to_all.22 = bf16[8,72,512]{2,1,0:T(8,128)(2,1)S(1)} all-to-all(bf16[8,72,512]{2,1,0:T(8,128)(2,1)S(1)} %broadcast_in_dim.2), channel_id=1, replica_groups=mesh['row'=8,'y'=4,'x'=4,'core'=2] {'row'}, dimensions={0} | all-to-all | bytes 1179648 | tf_op jit(solution)/shard_map/all_to_all | solution.py:262
  97.7 0.0 copy-start.1
  97.7 0.2 convolution_reduce_fusion
  98.0 3.0 %collective-permute-start.4 = (f32[3,512]{1,0:T(4,128)S(1)}, f32[3,512]{1,0:T(4,128)S(1)}, u32[]{:S(2)}, u32[]{:S(2)}) collective-permute-start(f32[3,512]{1,0:T(4,128)S(1)} %pad_maximum_fusion), channel_id=1, source_target_pairs={{0,1},{1,0},{2,3},{3,2},{4,5},{5,4},{6,7},{7,6},{8,9},{9,8},{10,11... | collective-permute-start | bytes 18440 | tf_op jit(solution)/shard_map/ppermute | solution.py:232
  101.0 0.1 collective-permute-start.3
  101.1 0.7 collective-permute-done.4
  101.9 0.1 fusion.13
  102.0 0.9 collective-permute-done.3.v_ref
  102.9 1.2 shard_map.78
  104.2 0.0 copy-done.1
  104.2 0.3 convert_element_type.141
  104.5 21.5 %all_to_all.23 = f16[16,72,512]{2,1,0:T(8,128)(2,1)S(1)} all-to-all(f16[16,72,512]{2,1,0:T(8,128)(2,1)S(1)} %convert_element_type.141), channel_id=1, replica_groups=mesh['row'=8,'y'=4,'x'=4,'core'=2] {'y','x'}, dimensions={0} | all-to-all | bytes 2359296 | tf_op jit(solution)/shard_map/all_to_all | solution.py:248
  125.9 0.3 convert_element_type.142
  126.2 0.1 fusion.6
  126.3 0.1 fusion.2
  126.4 0.9 fusion.raw_ref
  127.3 0.6 select_maximum_fusion.sums_ref
  127.9 7.6 %shard_map.79 = (f32[2048,512]{1,0:T(8,128)}, f32[64,512]{1,0:T(8,128)}, f32[2,512]{1,0:T(2,128)}) custom-call(bf16[2048,512]{1,0:T(8,128)(2,1)} %t_hbm.3, bf16[2,2048,512]{2,1,0:T(8,128)(2,1)} %f_hbm.3, bf16[512,512]{1,0:T(8,128)(2,1)} %bitcast.25, bf16[512,512]{1,0:T(8,128)(2,1)} %bitcast.29, f32[64,512]{1,0:T(8,128)} %fusion.raw_ref, ...), custom_call_target="tpu_custom_call" | custom-call | tf_op jit(solution)/shard_map/pallas_call | solution.py:181
  (27 shorter events, 0.5 us)
Async XLA Ops:
  2.0 9.2 %collective-permute-start = (bf16[1024,512]{1,0:T(8,128)(2,1)S(1)}, bf16[1024,512]{1,0:T(8,128)(2,1)S(1)}, u32[]{:S(2)}, u32[]{:S(2)}) collective-permute-start(bf16[1024,512]{1,0:T(8,128)(2,1)S(1)} %bitcast.31), channel_id=1, source_target_pairs={{0,1},{1,0},{2,3},{3,2},{4,5},{5,4},{6,7},{7,6},{8,9},{9,8},{10,11... | collective-permute-start | bytes 3145736 | tf_op jit(solution)/shard_map/ppermute | solution.py:215
  11.1 39.5 %copy-start.2 = (bf16[1024,512]{1,0:T(8,128)(2,1)S(1)}, bf16[1024,512]{1,0:T(8,128)(2,1)}, u32[]{:S(2)}) copy-start(bf16[1024,512]{1,0:T(8,128)(2,1)} %get-tuple-element.16.mine_ref) | copy-start | bytes 3145732
  48.5 3.5 %copy-start = (bf16[8,64,512]{2,1,0:T(8,128)(2,1)}, bf16[8,64,512]{2,1,0:T(8,128)(2,1)S(1)}, u32[]{:S(2)}) copy-start(bf16[8,64,512]{2,1,0:T(8,128)(2,1)S(1)} %slice.113) | copy-start | bytes 1572868
  48.5 2.2 %collective-permute-start.1 = (bf16[512,512]{1,0:T(8,128)(2,1)S(1)}, bf16[512,512]{1,0:T(8,128)(2,1)S(1)}, u32[]{:S(2)}, u32[]{:S(2)}) collective-permute-start(bf16[512,512]{1,0:T(8,128)(2,1)S(1)} %bitcast.22), channel_id=1, source_target_pairs={{0,1},{1,0},{2,3},{3,2},{4,5},{5,4},{6,7},{7,6},{8,9},{9,8},{10,11... | collective-permute-start | bytes 1572872 | tf_op jit(solution)/shard_map/ppermute | solution.py:229
  49.2 1.3 collective-permute-start.2
  77.2 0.9 copy-start.3
  77.2 1.0 copy-start.4
  97.7 6.4 %copy-start.1 = (bf16[8,64,512]{2,1,0:T(8,128)(2,1)}, bf16[8,64,512]{2,1,0:T(8,128)(2,1)S(1)}, u32[]{:S(2)}) copy-start(bf16[8,64,512]{2,1,0:T(8,128)(2,1)S(1)} %slice.121) | copy-start | bytes 1572868
  98.0 3.8 %collective-permute-start.4 = (f32[3,512]{1,0:T(4,128)S(1)}, f32[3,512]{1,0:T(4,128)S(1)}, u32[]{:S(2)}, u32[]{:S(2)}) collective-permute-start(f32[3,512]{1,0:T(4,128)S(1)} %pad_maximum_fusion), channel_id=1, source_target_pairs={{0,1},{1,0},{2,3},{3,2},{4,5},{5,4},{6,7},{7,6},{8,9},{9,8},{10,11... | collective-permute-start | bytes 18440 | tf_op jit(solution)/shard_map/ppermute | solution.py:232
  101.0 1.9 %collective-permute-start.3 = (bf16[512,512]{1,0:T(8,128)(2,1)S(1)}, bf16[512,512]{1,0:T(8,128)(2,1)S(1)}, u32[]{:S(2)}, u32[]{:S(2)}) collective-permute-start(bf16[512,512]{1,0:T(8,128)(2,1)S(1)} %bitcast.27), channel_id=1, source_target_pairs={{0,1},{1,0},{2,3},{3,2},{4,5},{5,4},{6,7},{7,6},{8,9},{9,8},{10,11... | collective-permute-start | bytes 1572872 | tf_op jit(solution)/shard_map/ppermute | solution.py:229

commit v3 on v2

--- a/solution.py
+++ b/solution.py
@@ -14,7 +14,9 @@
 EXTRA = 8
 TILE = 256
 CHUNK = 512
-NT = (((1,), (1,)), ((), ()))
+START = 50
+COUNTS = 52
+ANY = pl.BlockSpec(memory_space=pl.ANY)
 TN = (((0,), (0,)), ((), ()))
 WHOLE = pl.BlockSpec(memory_space=pltpu.VMEM)
 
@@ -39,9 +41,15 @@
     return jnp.pad(block, ((0, EXTRA - block.shape[0]), (0, 0)))
 
 
-def start_kernel(at_ref, t_hbm, f_hbm, e_hbm, b_hbm, tok_hbm, pay_ref, mine_ref, alpha_ref, seen_ref,
+def column():
+    core = lax.axis_index("core")
+    chip = lax.axis_index("y") * lax.axis_size("x") + lax.axis_index("x")
+    return core, chip * lax.axis_size("core") + core
+
+
+def start_kernel(t_hbm, f_hbm, e_hbm, b_hbm, tok_hbm, pay_ref, mine_ref, alpha_ref, seen_ref,
                  t_ref, f_ref, a_ref, e_ref, b_ref, tok_ref, g_ref, sems):
-    core, col = at_ref[0], at_ref[1]
+    core, col = column()
     piece = b_ref.shape[0]
     src = t_ref.shape[0]
     parts = src // CHUNK
@@ -99,7 +107,7 @@
         pay_ref[r] = jnp.concatenate([weights, part, tail], axis=0)
 
 
-def start_call(at, transitions, forward, emission, beta_end, token_ids, n_row):
+def start_call(transitions, forward, emission, beta_end, token_ids, n_row):
     src, dst = transitions.shape
     piece, seqs = beta_end.shape
     return pl.pallas_call(
@@ -110,7 +118,7 @@
             jax.ShapeDtypeStruct((piece, seqs), F32),
             jax.ShapeDtypeStruct((piece, seqs), F32),
         ),
-        in_specs=[pl.BlockSpec(memory_space=pltpu.SMEM)] + [pl.BlockSpec(memory_space=pl.ANY)] * 5,
+        in_specs=[pl.BlockSpec(memory_space=pl.ANY)] * 5,
         out_specs=(WHOLE,) * 4,
         scratch_shapes=[
             pltpu.VMEM((src, dst), BF16),
@@ -122,11 +130,20 @@
             pltpu.VMEM((dst, seqs), F32),
             pltpu.SemaphoreType.DMA((2 * (src // CHUNK) + 4,)),
         ],
-        compiler_params=params(56),
-    )(at, transitions, forward, emission, beta_end, token_ids)
-
-
-def product_kernel(mine_ref, other_ref, w_ref, v_ref, mul_ref, extra_ref, out_ref):
+        compiler_params=params(START),
+    )(transitions, forward, emission, beta_end, token_ids)
+
+
+def product_kernel(mine_ref, other_ref, w_ref, v_ref, mul_ref, extra_ref, *rest):
+    loads = []
+    if len(rest) == 1:
+        out_ref, = rest
+    else:
+        t_hbm, f_hbm, out_ref, t_ref, f_ref, sems = rest
+        for i, (source, target) in enumerate(((t_hbm, t_ref), (f_hbm, f_ref))):
+            loads.append(pltpu.make_async_copy(source, target, sems.at[i]))
+    for c in loads:
+        c.start()
     n_chip, rows, _ = out_ref.shape
     piece = rows - EXTRA
     mul = mul_ref[...]
@@ -140,6 +157,21 @@
         for j in range(group):
             out_ref[i * group + j, :piece, :] = part[j * piece:(j + 1) * piece]
             out_ref[i * group + j, piece:, :] = extra
+    for c in loads:
+        c.wait()
+
+
+def product_call(mine, other, w_own, w_other, mul, extra, n_chip, more):
+    rows, seqs = mine.shape[0] // n_chip, w_own.shape[1]
+    out = jax.ShapeDtypeStruct((n_chip, rows + EXTRA, seqs), F32)
+    return pl.pallas_call(
+        product_kernel,
+        out_shape=(out,) + tuple(jax.ShapeDtypeStruct(x.shape, x.dtype) for x in more),
+        in_specs=[WHOLE] * 6 + [ANY] * len(more),
+        out_specs=(WHOLE,) * (1 + len(more)),
+        scratch_shapes=[pltpu.SemaphoreType.DMA((2,))] if more else [],
+        compiler_params=params(16),
+    )(mine, other, w_own, w_other, mul, extra, *more)
 
 
 def counts_kernel(t_hbm, f_hbm, w1_ref, w0_ref, raw_ref, sums_ref, out_hbm, beta_ref, log_ref,
@@ -150,8 +182,8 @@
     for i in range(parts):
         rows = pl.ds(i * TILE, TILE)
         loads.append((
-            pltpu.make_async_copy(t_hbm.at[rows, :], t_ref.at[rows, :], sems.at[3 * i]),
-            pltpu.make_async_copy(f_hbm.at[:, rows, :], f_ref.at[:, rows, :], sems.at[3 * i + 1]),
+            pltpu.make_async_copy(f_hbm.at[:, rows, :], f_ref.at[:, rows, :], sems.at[3 * i]),
+            pltpu.make_async_copy(t_hbm.at[rows, :], t_ref.at[rows, :], sems.at[3 * i + 1]),
         ))
         stores.append(pltpu.make_async_copy(o_ref.at[rows, :], out_hbm.at[rows, :], sems.at[3 * i + 2]))
         for c in loads[i]:
@@ -160,7 +192,7 @@
     w0t_ref[...] = w0_ref[...].T
     beta_ref[...] = raw_ref[...] / sums_ref[2:3, :]
     log_ref[...] = jnp.log(sums_ref[2:4, :])
-    inv = 1.0 / sums_ref[0:2, :]
+    inv = (1.0 / seqs) / sums_ref[0:2, :]
     for i in range(parts):
         for c in loads[i]:
             c.wait()
@@ -169,7 +201,7 @@
         post0 = (f_ref[0, at, :].astype(F32) * inv[0:1]).astype(BF16)
         mixed = jnp.dot(post1, w1t_ref[...], preferred_element_type=F32)
         mixed = mixed + jnp.dot(post0, w0t_ref[...], preferred_element_type=F32)
-        o_ref[at, :] = t_ref[at, :].astype(F32) * (mixed * (1.0 / seqs))
+        o_ref[at, :] = t_ref[at, :].astype(F32) * mixed
         stores[i].start()
     for c in stores:
         c.wait()
@@ -185,8 +217,8 @@
             jax.ShapeDtypeStruct(raw.shape, F32),
             jax.ShapeDtypeStruct((steps, seqs), F32),
         ),
-        in_specs=[pl.BlockSpec(memory_space=pl.ANY)] * 2 + [WHOLE] * 4,
-        out_specs=(pl.BlockSpec(memory_space=pl.ANY), WHOLE, WHOLE),
+        in_specs=[ANY] * 2 + [WHOLE] * 4,
+        out_specs=(ANY, WHOLE, WHOLE),
         scratch_shapes=[
             pltpu.VMEM((src, dst), BF16),
             pltpu.VMEM((steps, src, seqs), BF16),
@@ -195,7 +227,7 @@
             pltpu.VMEM((seqs, dst), BF16),
             pltpu.SemaphoreType.DMA((3 * (src // TILE),)),
         ],
-        compiler_params=params(56),
+        compiler_params=params(COUNTS),
     )(transitions, forward, w1, w0, raw, sums)
 
 
@@ -207,15 +239,16 @@
     n_core = lax.axis_size("core")
     states = float(dst * n_chip * n_core)
     core = lax.axis_index("core")
-    col = (lax.axis_index("y") * lax.axis_size("x") + lax.axis_index("x")) * n_core + core
     swap = [(i, (i + 1) % n_core) for i in range(n_core)]
+
+    def spread(rows):
+        return jnp.broadcast_to(rows[None], (n_row,) + rows.shape)
 
     chunks = transitions.reshape(n_chip, n_core, piece, dst)
     theirs = lax.dynamic_index_in_dim(chunks, 1 - core, 1, keepdims=False).reshape(src // 2, dst)
     t_other = lax.ppermute(theirs, "core", swap)
-    at = jnp.stack([core, col]).astype(jnp.int32)
     pay, mine, alpha, observed = start_call(
-        at, transitions, forward, emission, beta_end, token_ids, n_row
+        transitions, forward, emission, beta_end, token_ids, n_row
     )
     pay, mine, t_other = lax.optimization_barrier((pay, mine, t_other))
 
@@ -225,7 +258,7 @@
     cs = jnp.sum(block[:, 2 * piece:2 * piece + 3].astype(F32), axis=(0, 1))
     cs = jnp.stack(split3(cs))
 
-    def backward(w_own, totals):
+    def backward(w_own, totals, more=()):
         w_other = lax.ppermute(w_own, "core", swap)
         sc = jnp.sum(jnp.dot(cs, w_own, preferred_element_type=F32), axis=0) / states / states
         own = jnp.stack([sc] + totals)
@@ -235,14 +268,9 @@
         rows = [power]
         for i in range(both.shape[0]):
             rows += split2(both[i] * down)
-        data = pl.pallas_call(
-            product_kernel,
-            out_shape=jax.ShapeDtypeStruct((n_chip, piece + EXTRA, seqs), F32),
-            in_specs=[WHOLE] * 6,
-            out_specs=WHOLE,
-            compiler_params=params(16),
-        )(mine, t_other, w_own, w_other, (down / states)[None, :], rows8(rows))
-        return data.astype(F16), both.shape[0]
+        mul = (down / states)[None, :]
+        data, *near = product_call(mine, t_other, w_own, w_other, mul, rows8(rows), n_chip, more)
+        return data.astype(F16), both.shape[0], near
 
     def collect(data, n):
         got = lax.all_to_all(data, CHIPS, 0, 0).astype(F32)
@@ -251,7 +279,7 @@
         sums = jnp.sum(got[:, piece + 1:] * up, axis=0)
         return raw, [sums[2 * i] + sums[2 * i + 1] for i in range(n)]
 
-    data, n = backward(w1, [])
+    data, n, _ = backward(w1, [])
     data, g_own = lax.optimization_barrier((data, g_own))
     raw, (scale1,) = collect(data, n)
 
@@ -259,12 +287,12 @@
     norm1 = jnp.sum(alpha * raw, axis=0) / states
     norm0 = jnp.sum(weights.astype(F32) * g_own, axis=0) / states / states
     pay = jnp.concatenate([weights, rows8(split3(norm1) + split3(norm0))], axis=0)
-    block = lax.all_to_all(jnp.broadcast_to(pay[None], (n_row,) + pay.shape), "row", 0, 0)
+    block = lax.all_to_all(spread(pay), "row", 0, 0)
     w0 = block[:, :piece].reshape(dst, seqs)
     sums = jnp.sum(block[:, piece:].astype(F32), axis=0)
     norm1 = sums[0] + sums[1] + sums[2]
     norm0 = sums[3] + sums[4] + sums[5]
-    data, n = backward(w0, [norm1, norm0])
+    data, n, _ = backward(w0, [norm1, norm0])
     raw, (scale0, norm1, norm0) = collect(data, n)
 
     sums = rows8([norm0, norm1, scale0, scale1])

time: 136 us -> 131 us (0.963)
  Pallas kernels: 15.2 us -> 13.1 us
  other arithmetic: 4.36 us -> 2.44 us
    pallas_call x1, Pallas kernels: 5.17 us -> 3.17 us  [start_call(): pl.pallas_call(start_kernel, out_shape=(jax.ShapeDtypeStruct((n_row, 2 *...]
  transfers between devices with their start and end apart: 5 -> 5, of which waited for: 3 -> 3; matrix products, arithmetic and copies ran while one was open for 1% -> 0% of each run, Pallas kernels for 4% -> 2%
where the time goes in v3:
time: 131 us
  blocking collectives  102 us (78%)
  Pallas kernels  13.1 us (10%)
  starting transfers between devices  7.12 us (5%)
  waiting for transfers between devices  2.91 us (2%)
  other arithmetic  2.44 us (2%)
  local copies, waits for them, and re-layouts  1.56 us (1%)
    all_to_all x2, blocking collectives, collect(): got = lax.all_to_all(data, CHIPS, 0, 0).astype(F32)  46 us
    all_to_all x1, blocking collectives, local(): block = lax.all_to_all(pay, 'row', 0, 0)  36.9 us
    all_to_all x1, blocking collectives, local(): block = lax.all_to_all(spread(pay), 'row', 0, 0)  19.3 us
    pallas_call x1, Pallas kernels, counts_call(): pl.pallas_call(counts_kernel, out_shape=(jax.ShapeDtypeStruct((src, dst),...  6.42 us
    pallas_call x2, Pallas kernels, product_call(): pl.pallas_call(product_kernel, out_shape=(out,) + tuple((jax.ShapeDtypeSt...  3.54 us
    ppermute x1, starting transfers between devices, local(): t_other = lax.ppermute(theirs, 'core', swap)  3.33 us
    pallas_call x1, Pallas kernels, start_call(): pl.pallas_call(start_kernel, out_shape=(jax.ShapeDtypeStruct((n_row, 2 *...  3.17 us
    ppermute x2, starting transfers between devices, backward(): both = own + lax.ppermute(own, 'core', swap)  3.13 us
  transfers between devices with their start and end apart: 5, of which 3 were waited for; matrix products, arithmetic and copies ran while one was open for 0% of the time, Pallas kernels for 2%

profile of v3, /device:TPU:1, one launch (start us, length us, event | category | flops | bytes accessed | tf_op | source)
XLA Modules:
  0.0 130.7 jit_solution(594908924572099231)
XLA Ops:
  0.6 0.0 copy-start.2
  0.6 0.0 copy-start.1
  0.7 0.0 copy-start
  0.7 1.4 %constant_dynamic-slice_fusion = bf16[16,1,64,512]{3,2,1,0:T(8,128)(2,1)S(1)} fusion(bf16[16,2,64,512]{3,2,1,0:T(8,128)(2,1)} %bitcast.28, s32[]{:T(128)S(6)} %select_n.4), kind=kLoop, calls=%fused_computation.74 | loop fusion | bytes 2097156 | tf_op jit(solution)/shard_map/jit(dynamic_index_in_dim)/dynamic_slice | solution.py:248
  2.0 3.3 %collective-permute-start = (bf16[1024,512]{1,0:T(8,128)(2,1)S(1)}, bf16[1024,512]{1,0:T(8,128)(2,1)S(1)}, u32[]{:S(2)}, u32[]{:S(2)}) collective-permute-start(bf16[1024,512]{1,0:T(8,128)(2,1)S(1)} %bitcast.29), channel_id=1, source_target_pairs={{0,1},{1,0},{2,3},{3,2},{4,5},{5,4},{6,7},{7,6},{8,9},{9,8},{10,11... | collective-permute-start | bytes 3145736 | tf_op jit(solution)/shard_map/ppermute | solution.py:249
  5.3 0.0 copy-done.2
  5.4 0.0 copy-done.1
  5.4 0.0 copy-done
  5.4 3.2 %shard_map.76 = (bf16[8,136,512]{2,1,0:T(8,128)(2,1)S(1)}, bf16[1024,512]{1,0:T(8,128)(2,1)S(1)}, f32[64,512]{1,0:T(8,128)S(1)}, f32[64,512]{1,0:T(8,128)S(1)}) custom-call(bf16[2048,512]{1,0:T(8,128)(2,1)} %t_hbm.3, bf16[2,2048,512]{2,1,0:T(8,128)(2,1)} %f_hbm.3, bf16[2,64,512]{2,1,0:T(8,128)(2,1)S(1)} %copy-done, f32[64,512]{1,0:T(8,128)S(1)} %copy-done.1, ...), custom_call_target="tpu_custom_call" | custom-call | tf_op jit(solution)/shard_map/pallas_call | solution.py:113
  8.5 0.0 collective-permute-done.other_ref
  8.5 36.9 %all_to_all.20 = bf16[8,136,512]{2,1,0:T(8,128)(2,1)S(1)} all-to-all(bf16[8,136,512]{2,1,0:T(8,128)(2,1)S(1)} %get-tuple-element.14), channel_id=1, replica_groups=mesh['row'=8,'y'=4,'x'=4,'core'=2] {'row'}, dimensions={0} | all-to-all | bytes 2228224 | tf_op jit(solution)/shard_map/all_to_all | solution.py:255
  45.5 0.6 collective-permute-start.1
  46.1 0.2 convolution_reduce_fusion.1
  46.3 0.1 collective-permute-start.2
  46.4 0.1 convert_reduce_fusion
  46.5 1.1 collective-permute-done.2
  47.7 0.0 collective-permute-done.1.v_ref
  47.7 1.2 shard_map.77
  49.0 0.3 convert_element_type.129
  49.3 24.6 %all_to_all.21 = f16[16,72,512]{2,1,0:T(8,128)(2,1)S(1)} all-to-all(f16[16,72,512]{2,1,0:T(8,128)(2,1)S(1)} %convert_element_type.129), channel_id=1, replica_groups=mesh['row'=8,'y'=4,'x'=4,'core'=2] {'y','x'}, dimensions={0} | all-to-all | bytes 2359296 | tf_op jit(solution)/shard_map/all_to_all | solution.py:276
  73.9 0.3 convert_element_type.131
  74.2 0.1 fusion.7
  74.3 0.1 fusion.3
  74.3 0.3 fusion.1
  74.6 0.1 multiply_reduce_fusion
  74.8 19.3 %all_to_all.22 = bf16[8,72,512]{2,1,0:T(8,128)(2,1)S(1)} all-to-all(bf16[8,72,512]{2,1,0:T(8,128)(2,1)S(1)} %broadcast_in_dim.2), channel_id=1, replica_groups=mesh['row'=8,'y'=4,'x'=4,'core'=2] {'row'}, dimensions={0} | all-to-all | bytes 1179648 | tf_op jit(solution)/shard_map/all_to_all | solution.py:290
  94.2 0.2 convolution_reduce_fusion
  94.4 3.0 %collective-permute-start.4 = (f32[3,512]{1,0:T(4,128)S(1)}, f32[3,512]{1,0:T(4,128)S(1)}, u32[]{:S(2)}, u32[]{:S(2)}) collective-permute-start(f32[3,512]{1,0:T(4,128)S(1)} %pad_maximum_fusion), channel_id=1, source_target_pairs={{0,1},{1,0},{2,3},{3,2},{4,5},{5,4},{6,7},{7,6},{8,9},{9,8},{10,11... | collective-permute-start | bytes 18440 | tf_op jit(solution)/shard_map/ppermute | solution.py:265
  97.4 0.1 collective-permute-start.3
  97.5 0.7 collective-permute-done.4
  98.3 0.1 fusion.13
  98.4 1.0 collective-permute-done.3.v_ref
  99.5 2.3 %shard_map.78 = f32[16,72,512]{2,1,0:T(8,128)S(1)} custom-call(bf16[1024,512]{1,0:T(8,128)(2,1)S(1)} %get-tuple-element.16.mine_ref, bf16[1024,512]{1,0:T(8,128)(2,1)S(1)} %collective-permute-done.other_ref, bf16[512,512]{1,0:T(8,128)(2,1)S(1)} %bitcast.26, bf16[512,512]{1,0:T(8,128)(2,1)} %collective-permute-done.3.v_ref, ...), custom_call_target="tpu_custom_call" | custom-call | tf_op jit(solution)/shard_map/pallas_call | solution.py:167
  101.8 0.3 convert_element_type.141
  102.1 21.5 %all_to_all.23 = f16[16,72,512]{2,1,0:T(8,128)(2,1)S(1)} all-to-all(f16[16,72,512]{2,1,0:T(8,128)(2,1)S(1)} %convert_element_type.141), channel_id=1, replica_groups=mesh['row'=8,'y'=4,'x'=4,'core'=2] {'y','x'}, dimensions={0} | all-to-all | bytes 2359296 | tf_op jit(solution)/shard_map/all_to_all | solution.py:276
  123.5 0.3 convert_element_type.142
  123.9 0.1 fusion.2
  124.0 0.3 fusion.raw_ref
  124.3 6.4 %shard_map.79 = (f32[2048,512]{1,0:T(8,128)}, f32[64,512]{1,0:T(8,128)}, f32[2,512]{1,0:T(2,128)}) custom-call(bf16[2048,512]{1,0:T(8,128)(2,1)} %t_hbm.3, bf16[2,2048,512]{2,1,0:T(8,128)(2,1)} %f_hbm.3, bf16[512,512]{1,0:T(8,128)(2,1)S(1)} %bitcast.23, bf16[512,512]{1,0:T(8,128)(2,1)S(1)} %bitcast.27, f32[64,512]{1,0:T(8,128)S(1)} %fusion.raw_ref, ...), custom_call_target="tpu_custom_call" | custom-call | tf_op jit(solution)/shard_map/pallas_call | solution.py:213
  (28 shorter events, 0.5 us)
Async XLA Ops:
  0.6 4.7 %copy-start.2 = (s32[2,512]{1,0:T(2,128)S(1)}, s32[2,512]{1,0:T(2,128)}, u32[]{:S(2)}) copy-start(s32[2,512]{1,0:T(2,128)} %tok_hbm.1) | copy-start | bytes 12292
  0.6 4.7 %copy-start.1 = (f32[64,512]{1,0:T(8,128)S(1)}, f32[64,512]{1,0:T(8,128)}, u32[]{:S(2)}) copy-start(f32[64,512]{1,0:T(8,128)} %b_hbm.1) | copy-start | bytes 393220
  0.7 4.7 %copy-start = (bf16[2,64,512]{2,1,0:T(8,128)(2,1)S(1)}, bf16[2,64,512]{2,1,0:T(8,128)(2,1)}, u32[]{:S(2)}) copy-start(bf16[2,64,512]{2,1,0:T(8,128)(2,1)} %e_hbm.1) | copy-start | bytes 393220
  2.0 6.5 %collective-permute-start = (bf16[1024,512]{1,0:T(8,128)(2,1)S(1)}, bf16[1024,512]{1,0:T(8,128)(2,1)S(1)}, u32[]{:S(2)}, u32[]{:S(2)}) collective-permute-start(bf16[1024,512]{1,0:T(8,128)(2,1)S(1)} %bitcast.29), channel_id=1, source_target_pairs={{0,1},{1,0},{2,3},{3,2},{4,5},{5,4},{6,7},{7,6},{8,9},{9,8},{10,11... | collective-permute-start | bytes 3145736 | tf_op jit(solution)/shard_map/ppermute | solution.py:249
  45.5 2.2 %collective-permute-start.1 = (bf16[512,512]{1,0:T(8,128)(2,1)S(1)}, bf16[512,512]{1,0:T(8,128)(2,1)S(1)}, u32[]{:S(2)}, u32[]{:S(2)}) collective-permute-start(bf16[512,512]{1,0:T(8,128)(2,1)S(1)} %bitcast.20), channel_id=1, source_target_pairs={{0,1},{1,0},{2,3},{3,2},{4,5},{5,4},{6,7},{7,6},{8,9},{9,8},{10,11... | collective-permute-start | bytes 1572872 | tf_op jit(solution)/shard_map/ppermute | solution.py:262
  46.3 1.3 %collective-permute-start.2 = (f32[1,512]{1,0:T(1,128)S(1)}, f32[1,512]{1,0:T(1,128)S(1)}, u32[]{:S(2)}, u32[]{:S(2)}) collective-permute-start(f32[1,512]{1,0:T(1,128)S(1)} %bitcast.35), channel_id=1, source_target_pairs={{0,1},{1,0},{2,3},{3,2},{4,5},{5,4},{6,7},{7,6},{8,9},{9,8},{10,11... | collective-permute-start | bytes 6152 | tf_op jit(solution)/shard_map/ppermute | solution.py:265
  94.4 3.8 %collective-permute-start.4 = (f32[3,512]{1,0:T(4,128)S(1)}, f32[3,512]{1,0:T(4,128)S(1)}, u32[]{:S(2)}, u32[]{:S(2)}) collective-permute-start(f32[3,512]{1,0:T(4,128)S(1)} %pad_maximum_fusion), channel_id=1, source_target_pairs={{0,1},{1,0},{2,3},{3,2},{4,5},{5,4},{6,7},{7,6},{8,9},{9,8},{10,11... | collective-permute-start | bytes 18440 | tf_op jit(solution)/shard_map/ppermute | solution.py:265
  97.4 2.0 %collective-permute-start.3 = (bf16[512,512]{1,0:T(8,128)(2,1)S(1)}, bf16[512,512]{1,0:T(8,128)(2,1)}, u32[]{:S(2)}, u32[]{:S(2)}) collective-permute-start(bf16[512,512]{1,0:T(8,128)(2,1)S(1)} %bitcast.25), channel_id=1, source_target_pairs={{0,1},{1,0},{2,3},{3,2},{4,5},{5,4},{6,7},{7,6},{8,9},{9,8},{10,11... | collective-permute-start | bytes 1572872 | tf_op jit(solution)/shard_map/ppermute | solution.py:262

commit v4 on v3

--- a/solution.py
+++ b/solution.py
@@ -15,8 +15,10 @@
 TILE = 256
 CHUNK = 512
 START = 50
+ROWS = 512
 COUNTS = 52
 ANY = pl.BlockSpec(memory_space=pl.ANY)
+NT = (((1,), (1,)), ((), ()))
 TN = (((0,), (0,)), ((), ()))
 WHOLE = pl.BlockSpec(memory_space=pltpu.VMEM)
 
@@ -175,12 +177,12 @@
 
 
 def counts_kernel(t_hbm, f_hbm, w1_ref, w0_ref, raw_ref, sums_ref, out_hbm, beta_ref, log_ref,
-                  t_ref, f_ref, o_ref, w1t_ref, w0t_ref, sems):
+                  t_ref, f_ref, o_ref, sems):
     src, seqs = f_ref.shape[1:]
-    parts = src // TILE
+    parts = src // ROWS
     loads, stores = [], []
     for i in range(parts):
-        rows = pl.ds(i * TILE, TILE)
+        rows = pl.ds(i * ROWS, ROWS)
         loads.append((
             pltpu.make_async_copy(f_hbm.at[:, rows, :], f_ref.at[:, rows, :], sems.at[3 * i]),
             pltpu.make_async_copy(t_hbm.at[rows, :], t_ref.at[rows, :], sems.at[3 * i + 1]),
@@ -188,19 +190,17 @@
         stores.append(pltpu.make_async_copy(o_ref.at[rows, :], out_hbm.at[rows, :], sems.at[3 * i + 2]))
         for c in loads[i]:
             c.start()
-    w1t_ref[...] = w1_ref[...].T
-    w0t_ref[...] = w0_ref[...].T
     beta_ref[...] = raw_ref[...] / sums_ref[2:3, :]
     log_ref[...] = jnp.log(sums_ref[2:4, :])
     inv = (1.0 / seqs) / sums_ref[0:2, :]
     for i in range(parts):
         for c in loads[i]:
             c.wait()
-        at = slice(i * TILE, (i + 1) * TILE)
+        at = slice(i * ROWS, (i + 1) * ROWS)
         post1 = (f_ref[1, at, :].astype(F32) * inv[1:2]).astype(BF16)
         post0 = (f_ref[0, at, :].astype(F32) * inv[0:1]).astype(BF16)
-        mixed = jnp.dot(post1, w1t_ref[...], preferred_element_type=F32)
-        mixed = mixed + jnp.dot(post0, w0t_ref[...], preferred_element_type=F32)
+        mixed = lax.dot_general(post1, w1_ref[...], NT, preferred_element_type=F32)
+        mixed = mixed + lax.dot_general(post0, w0_ref[...], NT, preferred_element_type=F32)
         o_ref[at, :] = t_ref[at, :].astype(F32) * mixed
         stores[i].start()
     for c in stores:
@@ -223,9 +223,7 @@
             pltpu.VMEM((src, dst), BF16),
             pltpu.VMEM((steps, src, seqs), BF16),
             pltpu.VMEM((src, dst), F32),
-            pltpu.VMEM((seqs, dst), BF16),
-            pltpu.VMEM((seqs, dst), BF16),
-            pltpu.SemaphoreType.DMA((3 * (src // TILE),)),
+            pltpu.SemaphoreType.DMA((3 * (src // ROWS),)),
         ],
         compiler_params=params(COUNTS),
     )(transitions, forward, w1, w0, raw, sums)

time: 131 us -> 131 us (level)
  no operation moved by 1% of the time
where the time goes in v4:
time: 131 us; the launch traced here: 130 us
  blocking collectives  102 us (78%)
  Pallas kernels  12.8 us (10%)
  starting transfers between devices  7.12 us (5%)
  waiting for transfers between devices  2.91 us (2%)
  other arithmetic  2.44 us (2%)
  local copies, waits for them, and re-layouts  1.56 us (1%)
    all_to_all x2, blocking collectives, collect(): got = lax.all_to_all(data, CHIPS, 0, 0).astype(F32)  46 us
    all_to_all x1, blocking collectives, local(): block = lax.all_to_all(pay, 'row', 0, 0)  36.9 us
    all_to_all x1, blocking collectives, local(): block = lax.all_to_all(spread(pay), 'row', 0, 0)  19.3 us
    pallas_call x1, Pallas kernels, counts_call(): pl.pallas_call(counts_kernel, out_shape=(jax.ShapeDtypeStruct((src, dst),...  6.08 us
    pallas_call x2, Pallas kernels, product_call(): pl.pallas_call(product_kernel, out_shape=(out,) + tuple((jax.ShapeDtypeSt...  3.54 us
    ppermute x1, starting transfers between devices, local(): t_other = lax.ppermute(theirs, 'core', swap)  3.33 us
    pallas_call x1, Pallas kernels, start_call(): pl.pallas_call(start_kernel, out_shape=(jax.ShapeDtypeStruct((n_row, 2 *...  3.17 us
    ppermute x2, starting transfers between devices, backward(): both = own + lax.ppermute(own, 'core', swap)  3.13 us
  transfers between devices with their start and end apart: 5, of which 3 were waited for; matrix products, arithmetic and copies ran while one was open for 0% of the time, Pallas kernels for 2%

profile of v4, /device:TPU:1, one launch (start us, length us, event | category | flops | bytes accessed | tf_op | source)
XLA Modules:
  0.0 130.4 jit_solution(11231133822721780199)
XLA Ops:
  0.6 0.0 copy-start.2
  0.6 0.0 copy-start.1
  0.7 0.0 copy-start
  0.7 1.4 %constant_dynamic-slice_fusion = bf16[16,1,64,512]{3,2,1,0:T(8,128)(2,1)S(1)} fusion(bf16[16,2,64,512]{3,2,1,0:T(8,128)(2,1)} %bitcast.28, s32[]{:T(128)S(6)} %select_n.4), kind=kLoop, calls=%fused_computation.74 | loop fusion | bytes 2097156 | tf_op jit(solution)/shard_map/jit(dynamic_index_in_dim)/dynamic_slice | solution.py:246
  2.0 3.3 %collective-permute-start = (bf16[1024,512]{1,0:T(8,128)(2,1)S(1)}, bf16[1024,512]{1,0:T(8,128)(2,1)S(1)}, u32[]{:S(2)}, u32[]{:S(2)}) collective-permute-start(bf16[1024,512]{1,0:T(8,128)(2,1)S(1)} %bitcast.29), channel_id=1, source_target_pairs={{0,1},{1,0},{2,3},{3,2},{4,5},{5,4},{6,7},{7,6},{8,9},{9,8},{10,11... | collective-permute-start | bytes 3145736 | tf_op jit(solution)/shard_map/ppermute | solution.py:247
  5.3 0.0 copy-done.2
  5.4 0.0 copy-done.1
  5.4 0.0 copy-done
  5.4 3.2 %shard_map.76 = (bf16[8,136,512]{2,1,0:T(8,128)(2,1)S(1)}, bf16[1024,512]{1,0:T(8,128)(2,1)S(1)}, f32[64,512]{1,0:T(8,128)S(1)}, f32[64,512]{1,0:T(8,128)S(1)}) custom-call(bf16[2048,512]{1,0:T(8,128)(2,1)} %t_hbm.3, bf16[2,2048,512]{2,1,0:T(8,128)(2,1)} %f_hbm.3, bf16[2,64,512]{2,1,0:T(8,128)(2,1)S(1)} %copy-done, f32[64,512]{1,0:T(8,128)S(1)} %copy-done.1, ...), custom_call_target="tpu_custom_call" | custom-call | tf_op jit(solution)/shard_map/pallas_call | solution.py:115
  8.5 0.0 collective-permute-done.other_ref
  8.5 36.9 %all_to_all.20 = bf16[8,136,512]{2,1,0:T(8,128)(2,1)S(1)} all-to-all(bf16[8,136,512]{2,1,0:T(8,128)(2,1)S(1)} %get-tuple-element.14), channel_id=1, replica_groups=mesh['row'=8,'y'=4,'x'=4,'core'=2] {'row'}, dimensions={0} | all-to-all | bytes 2228224 | tf_op jit(solution)/shard_map/all_to_all | solution.py:253
  45.5 0.6 collective-permute-start.1
  46.1 0.2 convolution_reduce_fusion.1
  46.3 0.1 collective-permute-start.2
  46.4 0.1 convert_reduce_fusion
  46.5 1.1 collective-permute-done.2
  47.7 0.0 collective-permute-done.1.v_ref
  47.7 1.2 shard_map.77
  49.0 0.3 convert_element_type.129
  49.3 24.6 %all_to_all.21 = f16[16,72,512]{2,1,0:T(8,128)(2,1)S(1)} all-to-all(f16[16,72,512]{2,1,0:T(8,128)(2,1)S(1)} %convert_element_type.129), channel_id=1, replica_groups=mesh['row'=8,'y'=4,'x'=4,'core'=2] {'y','x'}, dimensions={0} | all-to-all | bytes 2359296 | tf_op jit(solution)/shard_map/all_to_all | solution.py:274
  73.9 0.3 convert_element_type.131
  74.2 0.1 fusion.7
  74.3 0.1 fusion.3
  74.3 0.3 fusion.1
  74.6 0.1 multiply_reduce_fusion
  74.8 19.3 %all_to_all.22 = bf16[8,72,512]{2,1,0:T(8,128)(2,1)S(1)} all-to-all(bf16[8,72,512]{2,1,0:T(8,128)(2,1)S(1)} %broadcast_in_dim.2), channel_id=1, replica_groups=mesh['row'=8,'y'=4,'x'=4,'core'=2] {'row'}, dimensions={0} | all-to-all | bytes 1179648 | tf_op jit(solution)/shard_map/all_to_all | solution.py:288
  94.2 0.2 convolution_reduce_fusion
  94.4 3.0 %collective-permute-start.4 = (f32[3,512]{1,0:T(4,128)S(1)}, f32[3,512]{1,0:T(4,128)S(1)}, u32[]{:S(2)}, u32[]{:S(2)}) collective-permute-start(f32[3,512]{1,0:T(4,128)S(1)} %pad_maximum_fusion), channel_id=1, source_target_pairs={{0,1},{1,0},{2,3},{3,2},{4,5},{5,4},{6,7},{7,6},{8,9},{9,8},{10,11... | collective-permute-start | bytes 18440 | tf_op jit(solution)/shard_map/ppermute | solution.py:263
  97.4 0.1 collective-permute-start.3
  97.5 0.7 collective-permute-done.4
  98.3 0.1 fusion.13
  98.4 1.0 collective-permute-done.3.v_ref
  99.5 2.3 %shard_map.78 = f32[16,72,512]{2,1,0:T(8,128)S(1)} custom-call(bf16[1024,512]{1,0:T(8,128)(2,1)S(1)} %get-tuple-element.16.mine_ref, bf16[1024,512]{1,0:T(8,128)(2,1)S(1)} %collective-permute-done.other_ref, bf16[512,512]{1,0:T(8,128)(2,1)S(1)} %bitcast.26, bf16[512,512]{1,0:T(8,128)(2,1)} %collective-permute-done.3.v_ref, ...), custom_call_target="tpu_custom_call" | custom-call | tf_op jit(solution)/shard_map/pallas_call | solution.py:169
  101.8 0.3 convert_element_type.141
  102.1 21.5 %all_to_all.23 = f16[16,72,512]{2,1,0:T(8,128)(2,1)S(1)} all-to-all(f16[16,72,512]{2,1,0:T(8,128)(2,1)S(1)} %convert_element_type.141), channel_id=1, replica_groups=mesh['row'=8,'y'=4,'x'=4,'core'=2] {'y','x'}, dimensions={0} | all-to-all | bytes 2359296 | tf_op jit(solution)/shard_map/all_to_all | solution.py:274
  123.5 0.3 convert_element_type.142
  123.9 0.1 fusion.2
  124.0 0.3 fusion.raw_ref
  124.3 6.1 %shard_map.79 = (f32[2048,512]{1,0:T(8,128)}, f32[64,512]{1,0:T(8,128)}, f32[2,512]{1,0:T(2,128)}) custom-call(bf16[2048,512]{1,0:T(8,128)(2,1)} %t_hbm.3, bf16[2,2048,512]{2,1,0:T(8,128)(2,1)} %f_hbm.3, bf16[512,512]{1,0:T(8,128)(2,1)S(1)} %bitcast.23, bf16[512,512]{1,0:T(8,128)(2,1)S(1)} %bitcast.27, f32[64,512]{1,0:T(8,128)S(1)} %fusion.raw_ref, ...), custom_call_target="tpu_custom_call" | custom-call | tf_op jit(solution)/shard_map/pallas_call | solution.py:213
  (28 shorter events, 0.5 us)
Async XLA Ops:
  0.6 4.7 %copy-start.2 = (s32[2,512]{1,0:T(2,128)S(1)}, s32[2,512]{1,0:T(2,128)}, u32[]{:S(2)}) copy-start(s32[2,512]{1,0:T(2,128)} %tok_hbm.1) | copy-start | bytes 12292
  0.6 4.7 %copy-start.1 = (f32[64,512]{1,0:T(8,128)S(1)}, f32[64,512]{1,0:T(8,128)}, u32[]{:S(2)}) copy-start(f32[64,512]{1,0:T(8,128)} %b_hbm.1) | copy-start | bytes 393220
  0.7 4.7 %copy-start = (bf16[2,64,512]{2,1,0:T(8,128)(2,1)S(1)}, bf16[2,64,512]{2,1,0:T(8,128)(2,1)}, u32[]{:S(2)}) copy-start(bf16[2,64,512]{2,1,0:T(8,128)(2,1)} %e_hbm.1) | copy-start | bytes 393220
  2.0 6.5 %collective-permute-start = (bf16[1024,512]{1,0:T(8,128)(2,1)S(1)}, bf16[1024,512]{1,0:T(8,128)(2,1)S(1)}, u32[]{:S(2)}, u32[]{:S(2)}) collective-permute-start(bf16[1024,512]{1,0:T(8,128)(2,1)S(1)} %bitcast.29), channel_id=1, source_target_pairs={{0,1},{1,0},{2,3},{3,2},{4,5},{5,4},{6,7},{7,6},{8,9},{9,8},{10,11... | collective-permute-start | bytes 3145736 | tf_op jit(solution)/shard_map/ppermute | solution.py:247
  45.5 2.2 %collective-permute-start.1 = (bf16[512,512]{1,0:T(8,128)(2,1)S(1)}, bf16[512,512]{1,0:T(8,128)(2,1)S(1)}, u32[]{:S(2)}, u32[]{:S(2)}) collective-permute-start(bf16[512,512]{1,0:T(8,128)(2,1)S(1)} %bitcast.20), channel_id=1, source_target_pairs={{0,1},{1,0},{2,3},{3,2},{4,5},{5,4},{6,7},{7,6},{8,9},{9,8},{10,11... | collective-permute-start | bytes 1572872 | tf_op jit(solution)/shard_map/ppermute | solution.py:260
  46.3 1.3 %collective-permute-start.2 = (f32[1,512]{1,0:T(1,128)S(1)}, f32[1,512]{1,0:T(1,128)S(1)}, u32[]{:S(2)}, u32[]{:S(2)}) collective-permute-start(f32[1,512]{1,0:T(1,128)S(1)} %bitcast.35), channel_id=1, source_target_pairs={{0,1},{1,0},{2,3},{3,2},{4,5},{5,4},{6,7},{7,6},{8,9},{9,8},{10,11... | collective-permute-start | bytes 6152 | tf_op jit(solution)/shard_map/ppermute | solution.py:263
  94.4 3.8 %collective-permute-start.4 = (f32[3,512]{1,0:T(4,128)S(1)}, f32[3,512]{1,0:T(4,128)S(1)}, u32[]{:S(2)}, u32[]{:S(2)}) collective-permute-start(f32[3,512]{1,0:T(4,128)S(1)} %pad_maximum_fusion), channel_id=1, source_target_pairs={{0,1},{1,0},{2,3},{3,2},{4,5},{5,4},{6,7},{7,6},{8,9},{9,8},{10,11... | collective-permute-start | bytes 18440 | tf_op jit(solution)/shard_map/ppermute | solution.py:263
  97.4 2.0 %collective-permute-start.3 = (bf16[512,512]{1,0:T(8,128)(2,1)S(1)}, bf16[512,512]{1,0:T(8,128)(2,1)}, u32[]{:S(2)}, u32[]{:S(2)}) collective-permute-start(bf16[512,512]{1,0:T(8,128)(2,1)S(1)} %bitcast.25), channel_id=1, source_target_pairs={{0,1},{1,0},{2,3},{3,2},{4,5},{5,4},{6,7},{7,6},{8,9},{9,8},{10,11... | collective-permute-start | bytes 1572872 | tf_op jit(solution)/shard_map/ppermute | solution.py:260
